TPU v7x, 32 devices: a whole 2x2x4 slice. The times are simulated.
32 devices in a mesh: group: 2 (over x), node: 8 (over z, y), head: 2 (over core).
Axes of the slice: x: 2, y: 2, z: 4, core: 2. Of those that a mesh axis runs over, the one named last changes fastest.
Arguments:
- queries_one: bfloat16 [16, 128, 64, 128], P(('group', 'node'), None, 'head'), parts along dimension 0, may hold values from -80 to 80
- keys_one: bfloat16 [16, 128, 8, 128], P(('group', 'node'), None, 'head'), parts along dimension 0, may hold values from -8 to 8
- values_one: bfloat16 [16, 128, 8, 128], P(('group', 'node'), None, 'head'), parts along dimension 0, may hold values from -6 to 6
- queries_two: bfloat16 [16, 128, 64, 128], P(('group', 'node'), None, 'head'), parts along dimension 0, may hold values from -80 to 80
- keys_two: bfloat16 [16, 128, 8, 128], P(('group', 'node'), None, 'head'), parts along dimension 0, may hold values from -8 to 8
- values_two: bfloat16 [16, 128, 8, 128], P(('group', 'node'), None, 'head'), parts along dimension 0, may hold values from -6 to 6
- cache_keys: bfloat16 [512, 128, 8, 128], P(('group', 'node'), None, 'head'), parts along dimension 0, may hold values from -8 to 8
- cache_values: bfloat16 [512, 128, 8, 128], P(('group', 'node'), None, 'head'), parts along dimension 0, may hold values from -6 to 6
- paths: int32 [16, 32], P('group'), parts along dimension 0, may hold values from 0 to 255, as said below
- parents: int32 [16], P('group'), parts along dimension 0, may hold values from 0 to 7
- positions: int32 [2, 16, 128], P(None, ('group', 'node')), parts along dimension 1, may hold values from 0 to 8446, as said below
Outputs:
- attended_one: bfloat16 [16, 128, 64, 128], P(('group', 'node'), None, 'head'), parts along dimension 0
- attended_two: bfloat16 [16, 128, 64, 128], P(('group', 'node'), None, 'head'), parts along dimension 0
There are 2 independent parts, one for each index of `group`. A program takes and returns all parts, laid end to end along the dimension named above; each array names one. Nothing has to cross between parts.
Inputs may be any that keep to these rules, and one draw needn't show every extreme that they name: Each row paths[c] names 32 different cache blocks. Block b lies on device b // 32 of node, and each row names exactly 4 blocks of every device of node. positions[d, c, t] = s + (32 + d) * 128 + t, with one offset s of 0 to 4095 for a tree.
All inputs are finite; a program needn't handle non-finite values.
Results may differ from a plain program's by a relative error of at most 0.012.
The roundings to bfloat16 on the way count: a program that leaves them out, or rounds other values in their place, can miss the bound.
Values may be sent and summed in bfloat16 or wider, within the bound.
No kernel may reach another device: no remote copies, remote signals or barrier semaphores. Data moves between devices by JAX's collectives and lax.ppermute only.
A program may use at most 128 MiB of HBM per device.

v0:
```python
import functools

import jax
import jax.numpy as jnp
from jax import lax
from jax.experimental import pallas as pl
from jax.experimental.pallas import tpu as pltpu
from jax.sharding import PartitionSpec as P

rope_theta = 500000.0
log2_e = 1.4426950408889634
stat_rows = 32
row_tile = 256
vmem_bytes = 56 * 1024 * 1024


def rotary_tables(positions, head_width):
    half_width = head_width // 2
    place = jnp.arange(head_width, dtype=jnp.int32)
    pair = (place % half_width).astype(jnp.float32)
    frequency = rope_theta ** (-(pair * 2.0) / head_width)
    angles = positions.astype(jnp.float32)[..., None] * frequency
    return jnp.cos(angles), jnp.where(place < half_width, -1.0, 1.0) * jnp.sin(angles)


def rotary(vector, cosine, signed_sine):
    widened = vector.astype(jnp.float32)
    swapped = jnp.roll(widened, widened.shape[-1] // 2, axis=-1)
    turned = widened * cosine[:, None, :] + swapped * signed_sine[:, None, :]
    return turned.astype(jnp.bfloat16)


def turn_kernel(head_count, copies, first_ref, second_ref, cosine_ref, sine_ref, out_ref):
    token_tile, query_heads, width = first_ref.shape[1:]
    group_size = query_heads // head_count
    rows = token_tile * group_size
    for depth, query_ref in enumerate((first_ref, second_ref)):
        widened = query_ref[0].astype(jnp.float32)
        swapped = pltpu.roll(widened.reshape(token_tile * query_heads, width), width // 2, 1)
        swapped = swapped.reshape(token_tile, query_heads, width)
        turned = widened * cosine_ref[depth][:, None, :] + swapped * sine_ref[depth][:, None, :]
        for head in range(head_count):
            turned_head = turned[:, head * group_size : (head + 1) * group_size, :]
            turned_head = turned_head.reshape(rows, width).astype(jnp.bfloat16)
            for copy in range(copies):
                out_ref[copy * head_count + head, depth] = turned_head


def turn_queries(queries_one, queries_two, cosine, sine_part, head_count, copies):
    _, token_count, query_heads, width = queries_one.shape
    token_tile = 64
    rows = token_tile * query_heads // head_count
    query_spec = pl.BlockSpec((1, token_tile, query_heads, width), lambda step: (0, step, 0, 0))
    table_spec = pl.BlockSpec((2, token_tile, width), lambda step: (0, step, 0))
    return pl.pallas_call(
        functools.partial(turn_kernel, head_count, copies),
        grid=(token_count // token_tile,),
        in_specs=[query_spec, query_spec, table_spec, table_spec],
        out_specs=pl.BlockSpec(
            (head_count * copies, 2, rows, width), lambda step: (0, 0, step, 0)
        ),
        out_shape=jax.ShapeDtypeStruct(
            (head_count * copies, 2, token_count * query_heads // head_count, width), jnp.bfloat16
        ),
        compiler_params=pltpu.CompilerParams(vmem_limit_bytes=vmem_bytes),
        cost_estimate=pl.CostEstimate(
            flops=8 * queries_one.size, bytes_accessed=12 * queries_one.size, transcendentals=0
        ),
        name="turn_queries",
    )(queries_one, queries_two, cosine, sine_part)


def local_blocks(paths, here_index, per_owner, per_peer):
    is_local = paths // per_owner == here_index
    slot_rank = jnp.cumsum(is_local.astype(jnp.int32), axis=1) - 1
    slot_range = jnp.arange(per_peer, dtype=jnp.int32)
    selected = jnp.logical_and(
        is_local[:, :, None], slot_rank[:, :, None] == slot_range[None, None, :]
    )
    return jnp.sum(jnp.where(selected, (paths % per_owner)[:, :, None], 0), axis=1)


def pack_kernel(per_peer, head_count, token_count, near, index_ref, place_ref, *refs):
    key_refs = refs[:per_peer]
    value_refs = refs[per_peer : 2 * per_peer]
    new_refs = refs[2 * per_peer : 2 * per_peer + 2] if near else ()
    out_refs, wide = refs[-1 - head_count * (2 if near else 1) : -1], refs[-1]
    step = pl.program_id(0)
    mine = place_ref[0]
    span_rows = 2 * per_peer * token_count
    half = head_count // 2

    def spread(rows, put):
        wide[...] = rows.astype(jnp.float32)
        for far in range(head_count):
            head = lax.bitwise_xor(mine, far)
            picked = wide[pl.ds(head, token_count, stride=head_count), :]
            put(far, head, picked.astype(jnp.bfloat16))

    for which, source_refs in enumerate((key_refs, value_refs)):
        for slot, source in enumerate(source_refs):
            offset = (which * per_peer + slot) * token_count

            def put(far, head, rows):
                if not near:
                    start = pl.multiple_of(step * span_rows + offset, token_count)
                    out_refs[far][pl.ds(start, token_count), :] = rows
                    return
                apart = lax.bitwise_xor(step, head)
                start = pl.multiple_of((apart % half) * span_rows + offset, token_count)

                @pl.when(apart >= half)
                def _():
                    out_refs[far][pl.ds(start, token_count), :] = rows

                @pl.when(apart < half)
                def _():
                    out_refs[head_count + far][pl.ds(start, token_count), :] = rows

            spread(source[0], put)
    if near:

        @pl.when(step == 0)
        def _():
            for which, source in enumerate(new_refs):
                start = half * span_rows + which * token_count

                def put(far, head, rows):
                    out_refs[far][start : start + token_count, :] = rows

                spread(source[...], put)


def pack(cache_keys, cache_values, block_index, place, new_rows, per_peer, before=()):
    block_count, token_count, head_count, width = cache_keys.shape
    flat_keys = cache_keys.reshape(block_count, token_count * head_count, width)
    flat_values = cache_values.reshape(block_count, token_count * head_count, width)
    span_rows = 2 * per_peer * token_count
    near = bool(new_rows)
    half_rows = head_count // 2 * span_rows
    out_rows = half_rows + 2 * token_count if near else head_count * span_rows
    shapes = [(out_rows, width)] * head_count
    if near:
        shapes += [(half_rows, width)] * head_count

    def block_spec(slot):
        return pl.BlockSpec(
            (1, token_count * head_count, width),
            lambda step, index, place: (
                index[(place[1] * head_count + step) * per_peer + slot],
                0,
                0,
            ),
        )

    def whole_spec(shape):
        return pl.BlockSpec(shape, lambda step, index, place: (0,) * len(shape))

    cache_specs = [block_spec(slot) for slot in range(per_peer)]
    new_spec = pl.BlockSpec((token_count * head_count, width), lambda step, index, place: (0, 0))
    operands = [flat_keys] * per_peer + [flat_values] * per_peer
    operands += [row.reshape(token_count * head_count, width) for row in new_rows]
    return pl.pallas_call(
        functools.partial(pack_kernel, per_peer, head_count, token_count, near),
        grid_spec=pltpu.PrefetchScalarGridSpec(
            num_scalar_prefetch=2,
            grid=(head_count,),
            in_specs=cache_specs
            + cache_specs
            + [new_spec] * len(new_rows)
            + [pl.BlockSpec(memory_space=pl.ANY)] * len(before),
            out_specs=[whole_spec(shape) for shape in shapes],
            scratch_shapes=[pltpu.VMEM((token_count * head_count, width), jnp.float32)],
        ),
        out_shape=[jax.ShapeDtypeStruct(shape, jnp.bfloat16) for shape in shapes],
        compiler_params=pltpu.CompilerParams(vmem_limit_bytes=vmem_bytes),
        cost_estimate=pl.CostEstimate(
            flops=0, bytes_accessed=4 * head_count * out_rows * width, transcendentals=0
        ),
        name="pack_rows",
    )(block_index, place, *operands, *before)


def eye(size):
    return lax.broadcasted_iota(jnp.int32, (size, size), 0) == lax.broadcasted_iota(
        jnp.int32, (size, size), 1
    )


def product(left, right):
    return lax.dot_general(
        left, right, (((1,), (1,)), ((), ())), preferred_element_type=jnp.float32
    )


def fold_lanes(array, width, operation):
    pieces = [array[:, start : start + width] for start in range(0, array.shape[1], width)]
    while len(pieces) > 1:
        pieces = [
            operation(*pieces[start : start + 2]) if start + 1 < len(pieces) else pieces[start]
            for start in range(0, len(pieces), 2)
        ]
    return pieces[0]


def attend_task(query_of, put, row_count, width, parts, mask_of, level_ref, score_ref, score_scale):
    tile_count = row_count // row_tile

    def make_scores(tile):
        query = query_of(tile)
        top, start = None, 0
        for place, (keys, _) in enumerate(parts):
            scores = product(query, keys())
            if mask_of is not None and place == len(parts) - 1:
                scores = jnp.where(mask_of(tile), scores, -1e30)
            size = scores.shape[1]
            score_ref[tile % 2, :, start : start + size] = scores
            start += size
            folded = fold_lanes(scores, width, jnp.maximum)
            top = folded if top is None else jnp.maximum(top, folded)
        return jnp.max(top, axis=-1, keepdims=True)

    picks = eye(width)
    row_max = make_scores(0)
    for tile in range(tile_count):
        next_max = make_scores(tile + 1) if tile + 1 < tile_count else None
        total, mixture, start = None, None, 0
        for _, values in parts:
            value_rows = values()
            size = value_rows.shape[0]
            scores = score_ref[tile % 2, :, start : start + size]
            start += size
            weights = jnp.exp2((scores - row_max) * (score_scale * log2_e))
            folded = fold_lanes(weights, width, jnp.add)
            total = folded if total is None else total + folded
            mixed = jnp.dot(
                weights.astype(jnp.bfloat16), value_rows, preferred_element_type=jnp.float32
            )
            mixture = mixed if mixture is None else mixture + mixed
        total = jnp.sum(total, axis=-1, keepdims=True)
        put(tile * row_tile, (mixture / total).astype(jnp.bfloat16))
        level = row_max * score_scale + jnp.log(total)
        for piece in range(row_tile // width):
            line = jnp.where(picks, level[piece * width : (piece + 1) * width], 0.0)
            row = tile * (row_tile // width) + piece
            level_ref[row : row + 1, :] = jnp.sum(line, axis=0, keepdims=True)
        row_max = next_max
    levels = level_ref[...]
    high = levels.astype(jnp.bfloat16).astype(jnp.float32)
    middle = (levels - high).astype(jnp.bfloat16).astype(jnp.float32)
    low = levels - high - middle
    stats = jnp.concatenate([high, middle, low, jnp.zeros_like(levels)], 0)
    put(row_count, stats.astype(jnp.bfloat16))


def putter(out_ref):
    def put(start, rows):
        out_ref[start : start + rows.shape[0], :] = rows

    return put


def hand_out(stage_ref, out_refs):
    for far, out_ref in enumerate(out_refs):

        @pl.when(pl.program_id(0) == far)
        def _():
            out_ref[...] = stage_ref[...]


def tile_reader(query_ref):
    return lambda tile: query_ref[0, tile * row_tile : (tile + 1) * row_tile, :]


def task_scratch(row_count, width, key_count):
    return [
        pltpu.VMEM((row_count // width, width), jnp.float32),
        pltpu.VMEM((2, row_tile, key_count), jnp.float32),
    ]


def task_cost(task_count, row_count, key_count, width):
    return pl.CostEstimate(
        flops=4 * task_count * row_count * key_count * width,
        bytes_accessed=4 * task_count * (row_count + key_count) * width,
        transcendentals=task_count * row_count * key_count,
    )


def first_kernel(source_count, task_count, part_rows, score_scale, place_ref, query_ref, *refs):
    source_refs = refs[:source_count]
    out_refs = refs[-4 - task_count : -4]
    mark_ref, level_ref, score_ref, stage_ref = refs[-4:]
    _, row_count, width = query_ref.shape
    mark_ref[...] = jnp.zeros_like(mark_ref)
    parts = [
        (
            functools.partial(lambda ref: ref[0:part_rows, :], ref),
            functools.partial(lambda ref: ref[part_rows : 2 * part_rows, :], ref),
        )
        for ref in source_refs
    ]
    attend_task(
        tile_reader(query_ref),
        putter(stage_ref),
        row_count,
        width,
        parts,
        None,
        level_ref,
        score_ref,
        score_scale,
    )
    hand_out(stage_ref, out_refs)


def attend_first(queries, sources, place, task_of, slot_of, task_count, part_rows, score_scale, before):
    _, _, row_count, width = queries.shape
    out_rows = row_count + stat_rows
    span_rows = 2 * part_rows
    source_spec = pl.BlockSpec(
        (span_rows, width), lambda step, place: (slot_of(task_of(step), place), 0)
    )
    outs = pl.pallas_call(
        functools.partial(first_kernel, len(sources), task_count, part_rows, score_scale),
        grid_spec=pltpu.PrefetchScalarGridSpec(
            num_scalar_prefetch=1,
            grid=(task_count,),
            in_specs=[
                pl.BlockSpec(
                    (1, None, row_count, width),
                    lambda step, place: (lax.bitwise_xor(place[2], task_of(step)), 0, 0, 0),
                )
            ]
            + [source_spec] * len(sources)
            + [pl.BlockSpec(memory_space=pl.ANY)] * len(before),
            out_specs=[pl.BlockSpec((out_rows, width), lambda step, place: (0, 0))] * task_count
            + [pl.BlockSpec((8, width), lambda step, place: (0, 0))],
            scratch_shapes=task_scratch(row_count, width, len(sources) * part_rows)
            + [pltpu.VMEM((out_rows, width), jnp.bfloat16)],
        ),
        out_shape=[jax.ShapeDtypeStruct((out_rows, width), jnp.bfloat16)] * task_count
        + [jax.ShapeDtypeStruct((8, width), jnp.float32)],
        compiler_params=pltpu.CompilerParams(vmem_limit_bytes=vmem_bytes),
        cost_estimate=task_cost(task_count, row_count, len(sources) * part_rows, width),
        name="attend_first",
    )(place, queries, *sources, *before)
    return outs[:-1], (outs[-1],)


def second_kernel(
    head_count, far_chunks, task_of, task_count, part_rows, score_scale, parent_ref, place_ref, query_ref, *refs
):
    further_refs = refs[:head_count]
    nearer_refs = refs[head_count : 2 * head_count]
    far_refs = refs[2 * head_count : (2 + far_chunks) * head_count]
    out_refs = refs[-8 - task_count : -8]
    mark_ref, level_ref, score_ref, stage_ref, held, fresh = refs[-8:-2]
    semaphores, fresh_semaphores = refs[-2:]
    _, row_count, width = query_ref.shape
    span_rows = 2 * part_rows
    token_count = fresh.shape[1] // 2
    half = head_count // 2
    step = pl.program_id(0)
    node = place_ref[2]
    mark_ref[...] = jnp.zeros_like(mark_ref)

    def parent_at(number):
        return parent_ref[lax.bitwise_xor(node, task_of(number))]

    def fetch(number):
        parent = parent_at(number)
        apart = lax.bitwise_xor(parent, node)

        def bring(chosen, source_refs, slot):
            @pl.when(chosen)
            def _():
                rows = pl.ds(pl.multiple_of(slot * span_rows, span_rows), span_rows)
                for source in range(head_count):
                    pltpu.make_async_copy(
                        source_refs[source].at[rows],
                        held.at[number % 2, source],
                        semaphores.at[number % 2, source],
                    ).start()

        bring(apart < half, nearer_refs, apart)
        bring(jnp.logical_and(apart >= half, apart < head_count), further_refs, apart - half)
        for chunk in range(far_chunks):
            bring(
                apart // head_count == chunk + 1,
                far_refs[chunk * head_count : (chunk + 1) * head_count],
                parent % head_count,
            )

    @pl.when(step == 0)
    def _():
        fetch(0)
        fresh_copies = [
            pltpu.make_async_copy(
                further_refs[source].at[pl.ds(half * span_rows, 2 * token_count)],
                fresh.at[source],
                fresh_semaphores.at[source],
            )
            for source in range(head_count)
        ]
        for copy in fresh_copies:
            copy.start()
        for copy in fresh_copies:
            copy.wait()

    @pl.when(step + 1 < task_count)
    def _():
        fetch(step + 1)

    slot = step % 2
    for source in range(head_count):
        pltpu.make_async_copy(
            further_refs[source].at[pl.ds(0, span_rows)],
            held.at[slot, source],
            semaphores.at[slot, source],
        ).wait()
    apart = lax.bitwise_xor(parent_at(step), node)
    place = jnp.where(apart < head_count, apart, 0)
    parts = [
        (
            functools.partial(lambda source: held[slot, source, 0:part_rows, :], source),
            functools.partial(lambda source: held[slot, source, part_rows:span_rows, :], source),
        )
        for source in range(head_count)
    ]
    parts.append(
        (
            lambda: fresh[place, 0:token_count, :],
            lambda: fresh[place, token_count : 2 * token_count, :],
        )
    )

    def mask_of(tile):
        return jnp.broadcast_to(apart < head_count, (row_tile, token_count))

    attend_task(
        tile_reader(query_ref),
        putter(stage_ref),
        row_count,
        width,
        parts,
        mask_of,
        level_ref,
        score_ref,
        score_scale,
    )
    hand_out(stage_ref, out_refs)


def attend_second(
    queries, further, nearer, far, parents, place, task_of, task_count, part_rows, score_scale, before
):
    _, _, row_count, width = queries.shape
    head_count = len(further)
    span_rows = 2 * part_rows
    fresh_rows = further[0].shape[0] - head_count // 2 * span_rows
    keys = head_count * part_rows + fresh_rows // 2
    out_rows = row_count + stat_rows
    operands = [row for rows in (further, nearer, *far) for row in rows] + [*before]
    outs = pl.pallas_call(
        functools.partial(
            second_kernel, head_count, len(far), task_of, task_count, part_rows, score_scale
        ),
        grid_spec=pltpu.PrefetchScalarGridSpec(
            num_scalar_prefetch=2,
            grid=(task_count,),
            in_specs=[
                pl.BlockSpec(
                    (1, None, row_count, width),
                    lambda step, parent, place: (lax.bitwise_xor(place[2], task_of(step)), 1, 0, 0),
                )
            ]
            + [pl.BlockSpec(memory_space=pl.ANY)] * len(operands),
            out_specs=[pl.BlockSpec((out_rows, width), lambda step, parent, place: (0, 0))]
            * task_count
            + [pl.BlockSpec((8, width), lambda step, parent, place: (0, 0))],
            scratch_shapes=task_scratch(row_count, width, keys)
            + [
                pltpu.VMEM((out_rows, width), jnp.bfloat16),
                pltpu.VMEM((2, head_count, span_rows, width), jnp.bfloat16),
                pltpu.VMEM((head_count, fresh_rows, width), jnp.bfloat16),
                pltpu.SemaphoreType.DMA((2, head_count)),
                pltpu.SemaphoreType.DMA((head_count,)),
            ],
        ),
        out_shape=[jax.ShapeDtypeStruct((out_rows, width), jnp.bfloat16)] * task_count
        + [jax.ShapeDtypeStruct((8, width), jnp.float32)],
        compiler_params=pltpu.CompilerParams(vmem_limit_bytes=vmem_bytes),
        cost_estimate=task_cost(task_count, row_count, keys, width),
        name="attend_second",
    )(parents, place, queries, *operands)
    return outs[:-1], (outs[-1],)


def own_kernel(
    group_size, score_scale, place_ref, query_ref, key_ref, value_ref, out_ref, level_ref, score_ref
):
    token_count = key_ref.shape[1]
    _, row_count, width = query_ref.shape

    def mask_of(tile):
        row = tile * row_tile + lax.broadcasted_iota(jnp.int32, (row_tile, token_count), 0)
        column = lax.broadcasted_iota(jnp.int32, (row_tile, token_count), 1)
        return column * group_size <= row

    attend_task(
        tile_reader(query_ref),
        putter(out_ref.at[0]),
        row_count,
        width,
        [(lambda: key_ref[0], lambda: value_ref[0])],
        mask_of,
        level_ref,
        score_ref,
        score_scale,
    )


def attend_own(queries, depth, keys, values, place, score_scale):
    head_count, token_count, width = keys.shape
    row_count = queries.shape[2]

    def head_spec(rows):
        return pl.BlockSpec(
            (1, rows, width), lambda step, place: (lax.bitwise_xor(place[0], step), 0, 0)
        )

    return pl.pallas_call(
        functools.partial(own_kernel, row_count // token_count, score_scale),
        grid_spec=pltpu.PrefetchScalarGridSpec(
            num_scalar_prefetch=1,
            grid=(head_count,),
            in_specs=[
                pl.BlockSpec(
                    (1, None, row_count, width),
                    lambda step, place: (lax.bitwise_xor(place[0], step), depth, 0, 0),
                ),
                head_spec(token_count),
                head_spec(token_count),
            ],
            out_specs=pl.BlockSpec(
                (1, row_count + stat_rows, width), lambda step, place: (step, 0, 0)
            ),
            scratch_shapes=task_scratch(row_count, width, token_count),
        ),
        out_shape=jax.ShapeDtypeStruct((head_count, row_count + stat_rows, width), jnp.bfloat16),
        compiler_params=pltpu.CompilerParams(vmem_limit_bytes=vmem_bytes),
        cost_estimate=task_cost(head_count, row_count, token_count, width),
        name="attend_own",
    )(place, queries, keys, values)


def merge_kernel(head_count, group_size, part_count, place_ref, *refs):
    part_refs, own_ref = refs[:part_count], refs[part_count]
    refs = refs[part_count + 1 :]
    stat_refs, own_stat_ref = refs[:part_count], refs[part_count]
    out_ref, mixed_ref = refs[-2:]
    token_tile, _, lanes = out_ref.shape[1:]
    stat_tile = token_tile * group_size // lanes
    step = pl.program_id(0)
    picks = eye(lanes)
    ones = jnp.ones((2 * lanes, lanes), jnp.bfloat16)
    span = stat_rows // 4

    for far in range(head_count):
        head = lax.bitwise_xor(place_ref[0], far)
        sources = [part_refs[place] for place in range(far, part_count, head_count)]
        sources.append(own_ref.at[far])
        stats = [stat_refs[place][...] for place in range(far, part_count, head_count)]
        stats.append(own_stat_ref[far])
        stats = [stat.astype(jnp.float32) for stat in stats]
        level = [
            stat[:span] + stat[span : 2 * span] + stat[2 * span : 3 * span] for stat in stats
        ]
        top = functools.reduce(jnp.maximum, level)
        shares = [jnp.exp(one - top) for one in level]
        total = functools.reduce(jnp.add, shares)
        shares = [one / total for one in shares]
        lines = []
        for share in shares:
            for piece in range(stat_tile):
                chosen = (
                    lax.broadcasted_iota(jnp.int32, share.shape, 0) == step * stat_tile + piece
                )
                lines.append(jnp.sum(jnp.where(chosen, share, 0.0), axis=0, keepdims=True))
        scales = []
        for line in lines:
            high = line.astype(jnp.bfloat16).astype(jnp.float32)
            scales.append(
                jnp.concatenate(
                    [
                        jnp.where(picks, portion, 0.0).astype(jnp.bfloat16)
                        for portion in (high, line - high)
                    ],
                    1,
                )
            )
        columns = jnp.dot(
            jnp.concatenate(scales, 0), ones, preferred_element_type=jnp.float32
        )
        mixed = None
        rows = stat_tile * lanes
        for place, source in enumerate(sources):
            block = source[...].astype(jnp.float32) * columns[place * rows : (place + 1) * rows]
            mixed = block if mixed is None else mixed + block
        mixed_ref[
            :, pl.ds(pl.multiple_of(head * group_size, group_size), group_size), :
        ] = mixed.reshape(token_tile, group_size, lanes)
    out_ref[0] = mixed_ref[...].astype(out_ref.dtype)


def merge(parts, own, place, token_count, before=()):
    head_count, out_rows, width = own.shape
    row_count = out_rows - stat_rows
    group_size = row_count // token_count
    token_tile = 64
    rows = token_tile * group_size
    stat_block = row_count // stat_rows
    query_heads = head_count * group_size

    def specs(size, index):
        flat = pl.BlockSpec((size, width), lambda step, place: (index(step), 0))
        whole = pl.BlockSpec((head_count, size, width), lambda step, place: (0, index(step), 0))
        return [flat] * len(parts) + [whole]

    return pl.pallas_call(
        functools.partial(merge_kernel, head_count, group_size, len(parts)),
        grid_spec=pltpu.PrefetchScalarGridSpec(
            num_scalar_prefetch=1,
            grid=(token_count // token_tile,),
            in_specs=specs(rows, lambda step: step)
            + specs(stat_rows, lambda step: stat_block)
            + [pl.BlockSpec(memory_space=pl.ANY)] * len(before),
            out_specs=pl.BlockSpec(
                (1, token_tile, query_heads, width), lambda step, place: (0, step, 0, 0)
            ),
            scratch_shapes=[pltpu.VMEM((token_tile, query_heads, width), jnp.float32)],
        ),
        out_shape=jax.ShapeDtypeStruct((1, token_count, query_heads, width), jnp.bfloat16),
        compiler_params=pltpu.CompilerParams(vmem_limit_bytes=vmem_bytes),
        cost_estimate=pl.CostEstimate(
            flops=4 * (len(parts) + head_count) * row_count * width,
            bytes_accessed=4 * (len(parts) + head_count) * row_count * width,
            transcendentals=0,
        ),
        name="merge_parts",
    )(place, *parts, own, *parts, own, *before)


def local(
    queries_one,
    keys_one,
    values_one,
    queries_two,
    keys_two,
    values_two,
    cache_keys,
    cache_values,
    paths,
    parents,
    positions,
):
    here_index = lax.axis_index("node")
    peer_count = lax.axis_size("node")
    block_count, token_count, head_count, width = cache_keys.shape
    per_peer = paths.shape[1] // peer_count
    copies = peer_count // head_count
    score_scale = width ** (-0.5)
    my_head = here_index % head_count
    my_group = here_index // head_count
    part_rows = per_peer * token_count
    places = [
        jnp.stack([my_head, lax.bitwise_xor(my_group, apart), here_index])
        for apart in range(copies)
    ]

    def swap(array, apart):
        return lax.ppermute(array, "node", [(node, node ^ apart) for node in range(peer_count)])

    cosine, sine_part = rotary_tables(positions[:, 0], width)
    send = turn_queries(queries_one, queries_two, cosine, sine_part, head_count, copies)
    got = lax.all_to_all(send, "node", split_axis=0, concat_axis=0, tiled=True)
    key_rot_one = rotary(keys_one[0], cosine[0], sine_part[0])
    key_rot_two = rotary(keys_two[0], cosine[1], sine_part[1])

    block_index = local_blocks(paths, here_index, block_count, per_peer).reshape(-1)
    chunks = []
    before = (send,)
    for apart in range(1, copies):
        packed = pack(
            cache_keys, cache_values, block_index, places[apart], (), per_peer, before
        )
        chunks.append([packed[0]] + [swap(packed[far], far) for far in range(1, head_count)])
        before = (packed[0],)
    packed = pack(
        cache_keys,
        cache_values,
        block_index,
        places[0],
        (key_rot_one, values_one[0]),
        per_peer,
        before,
    )
    further = [packed[0]] + [swap(packed[far], far) for far in range(1, head_count)]
    nearer = [packed[head_count]] + [
        swap(packed[head_count + far], far) for far in range(1, head_count)
    ]

    own_one = attend_own(
        send,
        0,
        jnp.moveaxis(key_rot_one, 1, 0),
        jnp.moveaxis(values_one[0], 1, 0),
        places[0],
        score_scale,
    )
    own_two = attend_own(
        send,
        1,
        jnp.moveaxis(key_rot_two, 1, 0),
        jnp.moveaxis(values_two[0], 1, 0),
        places[0],
        score_scale,
    )

    half = head_count // 2
    parts_one, parts_two = [None] * peer_count, [None] * peer_count

    def send_home(parts, tasks, rows):
        for task, row in zip(tasks, rows):
            parts[task] = swap(row, task) if task else row

    def first(sources, tasks, task_of, slot_of, before):
        rows, before = attend_first(
            got,
            sources,
            places[0],
            task_of,
            slot_of,
            len(tasks),
            part_rows,
            score_scale,
            before,
        )
        send_home(parts_one, tasks, rows)
        return before

    def second(tasks, task_of, before):
        rows, before = attend_second(
            got,
            further,
            nearer,
            chunks,
            parents,
            places[0],
            task_of,
            len(tasks),
            part_rows,
            score_scale,
            before,
        )
        send_home(parts_two, tasks, rows)
        return before

    def far_slot(task, place):
        return lax.bitwise_xor(task % head_count, place[0])

    before = (own_one, own_two)
    for apart in range(1, copies):
        base = apart * head_count
        before = first(chunks[apart - 1], [base], lambda step: base, far_slot, before)
        before = first(
            chunks[apart - 1],
            list(range(base + 1, base + head_count)),
            lambda step: base + 1 + step,
            far_slot,
            before,
        )
    before = first(
        further,
        list(range(half, head_count)),
        lambda step: half + step,
        lambda task, place: task - half,
        before,
    )
    for apart in range(1, copies):
        base = apart * head_count
        before = second(
            list(range(base, base + head_count)), lambda step: base + step, before
        )
        before = (*before, *parts_one[base : base + head_count])
    before = first(
        nearer,
        list(range(1, half)) + [0],
        lambda step: (step + 1) % half,
        lambda task, place: task,
        (*before, *parts_one[half:head_count]),
    )
    before = second(
        list(range(1, head_count)),
        lambda step: step + 1,
        before,
    )
    before = second([0], lambda step: 0, before)
    before = (*before, *parts_two[head_count : head_count + 3])
    return (
        merge(parts_one, own_one, places[0], token_count, before),
        merge(parts_two, own_two, places[0], token_count),
    )


def solution(mesh):
    in_specs = (
        P(("group", "node"), None, "head", None),
        P(("group", "node"), None, "head", None),
        P(("group", "node"), None, "head", None),
        P(("group", "node"), None, "head", None),
        P(("group", "node"), None, "head", None),
        P(("group", "node"), None, "head", None),
        P(("group", "node"), None, "head", None),
        P(("group", "node"), None, "head", None),
        P("group", None),
        P("group"),
        P(None, ("group", "node"), None),
    )
    out_specs = (P(("group", "node"), None, "head", None), P(("group", "node"), None, "head", None))
    return jax.shard_map(
        local,
        mesh=mesh,
        in_specs=in_specs,
        out_specs=out_specs,
        check_vma=False,
    )
```

profile of v0, /device:TPU:0, one launch (start us, length us, event | category | flops | bytes accessed | tf_op | source)
XLA Modules:
  0.0 274.9 jit_solution(2482553521177080315)
XLA Ops:
  1.3 1.3 fusion.6
  2.6 3.8 %turn_queries.1.refs_8_.query_ref = bf16[8,2,1024,128]{3,2,1,0:T(8,128)(2,1)} custom-call(bf16[1,128,32,128]{3,2,1,0:T(8,128)(2,1)} %first_ref.1, bf16[1,128,32,128]{3,2,1,0:T(8,128)(2,1)} %second_ref.1, f32[2,128,128]{2,1,0:T(8,128)} %get-tuple-element.85.cosine_ref, f32[2,128,128]{2,1,0:T(8,128)} %get-tuple-element.84.sine_ref), custom_call_target="tpu_custom_call" | custom-call | flops 4194304 | bytes 6291456 | tf_op jit(solution)/shard_map/turn_queries/pallas_call | solution.py:55
  6.4 7.4 %all-to-all-start = ((bf16[8,2,1024,128]{3,2,1,0:T(8,128)(2,1)}), bf16[8,2,1024,128]{3,2,1,0:T(8,128)(2,1)}, u32[]{:S(2)}, u32[]{:S(2)}) async-start(bf16[8,2,1024,128]{3,2,1,0:T(8,128)(2,1)} %turn_queries.1.refs_8_.query_ref), calls=%async_computation | async-start | bytes 8388608 | tf_op jit(solution)/shard_map/all_to_all | solution.py:687
  15.6 7.1 %pack_rows.2 = (bf16[4096,128]{1,0:T(8,128)(2,1)}, bf16[4096,128]{1,0:T(8,128)(2,1)}, bf16[4096,128]{1,0:T(8,128)(2,1)}, bf16[4096,128]{1,0:T(8,128)(2,1)}) custom-call(s32[32]{0:T(128)} %reshape.65.index_ref, s32[3]{0:T(128)} %add_add_fusion.1.place_ref, bf16[32,512,128]{2,1,0:T(8,128)(2,1)} %bitcast.44, bf16[32,512,128]{2,1,0:T(8,128)(2,1)} %bitcast.45, ...), custom_call_target="tpu_custom_call" | custom-call | bytes 8388608 | tf_op jit(solution)/shard_map/pack_rows/pallas_call | solution.py:163
  22.6 1.9 collective-permute-start.6
  24.6 1.5 collective-permute-start.7
  27.0 0.8 fusion.1.refs_8_
  28.3 7.6 %pack_rows.3 = (bf16[2304,128]{1,0:T(8,128)(2,1)}, bf16[2304,128]{1,0:T(8,128)(2,1)}, bf16[2304,128]{1,0:T(8,128)(2,1)}, bf16[2304,128]{1,0:T(8,128)(2,1)}, bf16...) custom-call(s32[32]{0:T(128)} %reshape.65.index_ref, ...), custom_call_target="tpu_custom_call" | custom-call | bytes 4718592 | tf_op jit(solution)/shard_map/pack_rows/pallas_call | solution.py:163
  36.0 1.9 collective-permute-start.3
  37.9 1.6 collective-permute-start.4
  41.0 0.8 fusion.7.key_ref
  41.8 5.2 %attend_own.3.refs_5_.refs_8_.refs_17_ = bf16[4,1056,128]{2,1,0:T(8,128)(2,1)} custom-call(s32[3]{0:T(128)} %add_add_fusion.place_ref, bf16[8,2,1024,128]{3,2,1,0:T(8,128)(2,1)} %turn_queries.1.refs_8_.query_ref, bf16[4,128,128]{2,1,0:T(8,128)(2,1)} %fusion.7.key_ref, bf16[4,128,128]{2,1,0:T(8,128)(2,1)} %bitcast.67), custom_call_target="tpu_custom_call" | custom-call | flops 268435456 | bytes 2359296 | tf_op jit(solution)/shard_map/attend_own/pallas_call | solution.py:533
  47.0 50.0 %collective-permute-done.3.refs_1_ = bf16[2304,128]{1,0:T(8,128)(2,1)S(1)} collective-permute-done((bf16[2304,128]{1,0:T(8,128)(2,1)}, bf16[2304,128]{1,0:T(8,128)(2,1)S(1)}, u32[]{:S(2)}, u32[]{:S(2)}) %collective-permute-start.3) | collective-permute-done | bytes 589856 | tf_op jit(solution)/shard_map/ppermute | solution.py:683
  97.7 0.8 fusion.8.key_ref
  98.5 5.2 %attend_own.2.refs_4_.refs_8_.refs_17_ = bf16[4,1056,128]{2,1,0:T(8,128)(2,1)} custom-call(s32[3]{0:T(128)} %add_add_fusion.place_ref, bf16[8,2,1024,128]{3,2,1,0:T(8,128)(2,1)} %turn_queries.1.refs_8_.query_ref, bf16[4,128,128]{2,1,0:T(8,128)(2,1)} %fusion.8.key_ref, bf16[4,128,128]{2,1,0:T(8,128)(2,1)} %bitcast.66), custom_call_target="tpu_custom_call" | custom-call | flops 268435456 | bytes 2359296 | tf_op jit(solution)/shard_map/attend_own/pallas_call | solution.py:533
  103.7 0.9 collective-permute-start
  104.6 2.9 %collective-permute-done.7.refs_2_.refs_10_ = bf16[4096,128]{1,0:T(8,128)(2,1)S(1)} collective-permute-done((bf16[4096,128]{1,0:T(8,128)(2,1)}, bf16[4096,128]{1,0:T(8,128)(2,1)S(1)}, u32[]{:S(2)}, u32[]{:S(2)}) %collective-permute-start.7) | collective-permute-done | bytes 1048608 | tf_op jit(solution)/shard_map/ppermute | solution.py:683
  107.5 1.1 collective-permute-start.1
  108.6 22.0 %collective-permute-done.8.refs_3_.refs_11_ = bf16[4096,128]{1,0:T(8,128)(2,1)S(1)} collective-permute-done((bf16[4096,128]{1,0:T(8,128)(2,1)}, bf16[4096,128]{1,0:T(8,128)(2,1)S(1)}, u32[]{:S(2)}, u32[]{:S(2)}) %collective-permute-start.8) | collective-permute-done | bytes 1048608 | tf_op jit(solution)/shard_map/ppermute | solution.py:683
  130.6 1.4 collective-permute-start.2
  132.0 5.8 %attend_first.4 = (bf16[1056,128]{1,0:T(8,128)(2,1)}, f32[8,128]{1,0:T(8,128)}) custom-call(s32[3]{0:T(128)} %add_add_fusion.place_ref, bf16[8,2,1024,128]{3,2,1,0:T(8,128)(2,1)} %all-to-all-done.query_ref, bf16[4096,128]{1,0:T(8,128)(2,1)} %get-tuple-element.37.refs_10_.refs_0_.refs_8_, bf16[4096,128]{1,0:T(8,128)(2,1)} %copy-done, ...), custom_call_target="tpu_custom_call" | custom-call | flops 1073741824 | bytes 1572864 | tf_op jit(solution)/shard_map/attend_first/pallas_call | solution.py:324
  137.8 5.0 %collective-permute-done.4.refs_2_ = bf16[2304,128]{1,0:T(8,128)(2,1)} collective-permute-done((bf16[2304,128]{1,0:T(8,128)(2,1)}, bf16[2304,128]{1,0:T(8,128)(2,1)}, u32[]{:S(2)}, u32[]{:S(2)}) %collective-permute-start.4) | collective-permute-done | bytes 589856 | tf_op jit(solution)/shard_map/ppermute | solution.py:683
  142.8 2.5 collective-permute-start.9
  145.3 12.1 %attend_first.5 = (bf16[1056,128]{1,0:T(8,128)(2,1)}, bf16[1056,128]{1,0:T(8,128)(2,1)}, bf16[1056,128]{1,0:T(8,128)(2,1)}, f32[8,128]{1,0:T(8,128)}) custom-call(s32[3]{0:T(128)} %add_add_fusion.place_ref, bf16[8,2,1024,128]{3,2,1,0:T(8,128)(2,1)} %all-to-all-done.query_ref, bf16[4096,128]{1,0:T(8,128)(2,1)} %get-tuple-element.37.refs_10_.refs_0_.refs_8_, ...), custom_call_target="tpu_custom_call" | custom-call | flops 3221225472 | bytes 4718592 | tf_op jit(solution)/shard_map/attend_first/pallas_call | solution.py:324
  157.4 4.3 %collective-permute-done.5.refs_3_ = bf16[2304,128]{1,0:T(8,128)(2,1)} collective-permute-done((bf16[2304,128]{1,0:T(8,128)(2,1)}, bf16[2304,128]{1,0:T(8,128)(2,1)}, u32[]{:S(2)}, u32[]{:S(2)}) %collective-permute-start.5) | collective-permute-done | bytes 589856 | tf_op jit(solution)/shard_map/ppermute | solution.py:683
  161.8 0.8 collective-permute-start.10
  162.5 9.0 %attend_first.6 = (bf16[1056,128]{1,0:T(8,128)(2,1)}, bf16[1056,128]{1,0:T(8,128)(2,1)}, f32[8,128]{1,0:T(8,128)}) custom-call(s32[3]{0:T(128)} %add_add_fusion.place_ref, bf16[8,2,1024,128]{3,2,1,0:T(8,128)(2,1)} %all-to-all-done.query_ref, bf16[2304,128]{1,0:T(8,128)(2,1)} %get-tuple-element.42.refs_0_, bf16[2304,128]{1,0:T(8,128)(2,1)} %copy-done.6, ...), custom_call_target="tpu_custom_call" | custom-call | flops 2147483648 | bytes 3145728 | tf_op jit(solution)/shard_map/attend_first/pallas_call | solution.py:324
  171.5 2.0 collective-permute-start.11
  173.5 4.7 %collective-permute-done.1.refs_6_.refs_2_ = bf16[2048,128]{1,0:T(8,128)(2,1)} collective-permute-done((bf16[2048,128]{1,0:T(8,128)(2,1)}, bf16[2048,128]{1,0:T(8,128)(2,1)}, u32[]{:S(2)}, u32[]{:S(2)}) %collective-permute-start.1) | collective-permute-done | bytes 524320 | tf_op jit(solution)/shard_map/ppermute | solution.py:683
  178.3 3.2 %collective-permute-start.12 = (bf16[1056,128]{1,0:T(8,128)(2,1)S(1)}, bf16[1056,128]{1,0:T(8,128)(2,1)S(1)}, u32[]{:S(2)}, u32[]{:S(2)}) collective-permute-start(bf16[1056,128]{1,0:T(8,128)(2,1)S(1)} %copy-done.25), channel_id=1, source_target_pairs={{0,14},{2,12},{4,10},{6,8},{8,6},{10,4},{12,2},{14,0},{1,15},{3,13... | collective-permute-start | bytes 811016 | tf_op jit(solution)/shard_map/ppermute | solution.py:683
  181.5 7.5 %collective-permute-done.2.refs_7_.refs_3_ = bf16[2048,128]{1,0:T(8,128)(2,1)} collective-permute-done((bf16[2048,128]{1,0:T(8,128)(2,1)}, bf16[2048,128]{1,0:T(8,128)(2,1)}, u32[]{:S(2)}, u32[]{:S(2)}) %collective-permute-start.2) | collective-permute-done | bytes 524320 | tf_op jit(solution)/shard_map/ppermute | solution.py:683
  189.0 2.0 collective-permute-start.14
  191.0 18.0 %attend_second.3 = (bf16[1056,128]{1,0:T(8,128)(2,1)}, bf16[1056,128]{1,0:T(8,128)(2,1)}, bf16[1056,128]{1,0:T(8,128)(2,1)}, bf16[1056,128]{1,0:T(8,128)(2,1)}, f32[8,128]{1,0:T(8,128)}) custom-call(s32[8]{0:T(128)} %parent_ref.5, s32[3]{0:T(128)} %add_add_fusion.place_ref, bf16[8,2,1024,128]{3,2,1,0:T(8,128)(2,1)} %all-to-all-done.query_ref, ...), custom_call_target="tpu_custom_call" | custom-call | flops 4563402752 | bytes 6553600 | tf_op jit(solution)/shard_map/attend_second/pallas_call | solution.py:465
  209.1 1.7 collective-permute-start.16
  210.8 2.2 collective-permute-start.17
  213.0 3.1 %collective-permute-start.18 = (bf16[1056,128]{1,0:T(8,128)(2,1)}, bf16[1056,128]{1,0:T(8,128)(2,1)S(1)}, u32[]{:S(2)}, u32[]{:S(2)}) collective-permute-start(bf16[1056,128]{1,0:T(8,128)(2,1)} %get-tuple-element.66), channel_id=1, source_target_pairs={{0,12},{2,14},{4,8},{6,10},{8,4},{10,6},{12,0},{14,2},{1,13},{3,15... | collective-permute-start | bytes 811016 | tf_op jit(solution)/shard_map/ppermute | solution.py:683
  216.0 0.8 collective-permute-start.22
  216.8 0.7 copy-done.14
  217.5 8.9 %attend_first.7 = (bf16[1056,128]{1,0:T(8,128)(2,1)}, bf16[1056,128]{1,0:T(8,128)(2,1)}, f32[8,128]{1,0:T(8,128)}) custom-call(s32[3]{0:T(128)} %add_add_fusion.place_ref, bf16[8,2,1024,128]{3,2,1,0:T(8,128)(2,1)} %all-to-all-done.query_ref, bf16[2048,128]{1,0:T(8,128)(2,1)} %get-tuple-element.38.refs_4_.refs_0_, ...), custom_call_target="tpu_custom_call" | custom-call | flops 2147483648 | bytes 3145728 | tf_op jit(solution)/shard_map/attend_first/pallas_call | solution.py:324
  226.4 1.5 collective-permute-start.15
  227.9 14.5 %attend_second.4 = (bf16[1056,128]{1,0:T(8,128)(2,1)}, bf16[1056,128]{1,0:T(8,128)(2,1)}, bf16[1056,128]{1,0:T(8,128)(2,1)}, f32[8,128]{1,0:T(8,128)}) custom-call(s32[8]{0:T(128)} %parent_ref.5, s32[3]{0:T(128)} %add_add_fusion.place_ref, bf16[8,2,1024,128]{3,2,1,0:T(8,128)(2,1)} %all-to-all-done.query_ref, bf16[2304,128]{1,0:T(8,128)(2,1)} %get-tuple-element.42.refs_0_, ...), custom_call_target="tpu_custom_call" | custom-call | flops 3422552064 | bytes 4915200 | tf_op jit(solution)/shard_map/attend_second/pallas_call | solution.py:465
  242.6 1.2 collective-permute-start.19
  243.8 5.2 %collective-permute-done.17.refs_20_.refs_5_.refs_14_ = bf16[1056,128]{1,0:T(8,128)(2,1)S(1)} collective-permute-done((bf16[1056,128]{1,0:T(8,128)(2,1)}, bf16[1056,128]{1,0:T(8,128)(2,1)S(1)}, u32[]{:S(2)}, u32[]{:S(2)}) %collective-permute-start.17) | collective-permute-done | bytes 270368 | tf_op jit(solution)/shard_map/ppermute | solution.py:683
  249.0 6.3 %collective-permute-start.21 = (bf16[1056,128]{1,0:T(8,128)(2,1)}, bf16[1056,128]{1,0:T(8,128)(2,1)S(1)}, u32[]{:S(2)}, u32[]{:S(2)}) collective-permute-start(bf16[1056,128]{1,0:T(8,128)(2,1)} %get-tuple-element.70), channel_id=1, source_target_pairs={{0,6},{2,4},{4,2},{6,0},{8,14},{10,12},{12,10},{14,8},{1,7},{3,5},... | collective-permute-start | bytes 811016 | tf_op jit(solution)/shard_map/ppermute | solution.py:683
  255.4 7.1 %attend_second.5 = (bf16[1056,128]{1,0:T(8,128)(2,1)}, f32[8,128]{1,0:T(8,128)}) custom-call(s32[8]{0:T(128)} %parent_ref.5, s32[3]{0:T(128)} %add_add_fusion.place_ref, bf16[8,2,1024,128]{3,2,1,0:T(8,128)(2,1)} %all-to-all-done.query_ref, bf16[2304,128]{1,0:T(8,128)(2,1)} %get-tuple-element.42.refs_0_, bf16[2304,128]{1,0:T(8,128)(2,1)} %copy-done.6, ...), custom_call_target="tpu_custom_call" | custom-call | flops 1140850688 | bytes 1638400 | tf_op jit(solution)/shard_map/attend_second/pallas_call | solution.py:465
  262.5 0.7 copy-done.15
  263.2 5.2 %merge_parts.2 = bf16[1,128,32,128]{3,2,1,0:T(8,128)(2,1)} custom-call(s32[3]{0:T(128)} %add_add_fusion.place_ref, bf16[1056,128]{1,0:T(8,128)(2,1)} %get-tuple-element.59.refs_0_.refs_9_, bf16[1056,128]{1,0:T(8,128)(2,1)} %copy-done.15, bf16[1056,128]{1,0:T(8,128)(2,1)} %copy-done.13, bf16[1056,128]{1,0:T(8,128)(2,1)} %copy-done.14, ...), custom_call_target="tpu_custom_call" | custom-call | flops 6291456 | bytes 6291456 | tf_op jit(solution)/shard_map/merge_parts/pallas_call | solution.py:631
  269.5 5.2 %merge_parts.3 = bf16[1,128,32,128]{3,2,1,0:T(8,128)(2,1)} custom-call(s32[3]{0:T(128)} %add_add_fusion.place_ref, bf16[1056,128]{1,0:T(8,128)(2,1)} %get-tuple-element.67.refs_0_.refs_9_, bf16[1056,128]{1,0:T(8,128)(2,1)} %copy-done.17, bf16[1056,128]{1,0:T(8,128)(2,1)} %copy-done.18, bf16[1056,128]{1,0:T(8,128)(2,1)} %copy-done.19, ...), custom_call_target="tpu_custom_call" | custom-call | flops 6291456 | bytes 6291456 | tf_op jit(solution)/shard_map/merge_parts/pallas_call | solution.py:631
  (95 shorter events, 7.1 us)
Async XLA Ops:
  6.4 7.4 %copy-start.24 = (s32[8,32]{1,0:T(8,128)S(1)}, s32[8,32]{1,0:T(8,128)}, u32[]{:S(2)}) copy-start(s32[8,32]{1,0:T(8,128)} %param.19) | copy-start | bytes 3076
  6.4 125.6 %all-to-all-start = ((bf16[8,2,1024,128]{3,2,1,0:T(8,128)(2,1)}), bf16[8,2,1024,128]{3,2,1,0:T(8,128)(2,1)}, u32[]{:S(2)}, u32[]{:S(2)}) async-start(bf16[8,2,1024,128]{3,2,1,0:T(8,128)(2,1)} %turn_queries.1.refs_8_.query_ref), calls=%async_computation | async-start | bytes 8388608 | tf_op jit(solution)/shard_map/all_to_all | solution.py:687
  15.5 10.6 %copy-start.22 = (bf16[1,128,4,128]{3,2,1,0:T(4,128)(2,1)S(1)}, bf16[1,128,4,128]{3,2,1,0:T(4,128)(2,1)}, u32[]{:S(2)}) copy-start(bf16[1,128,4,128]{3,2,1,0:T(4,128)(2,1)} %param.12) | copy-start | bytes 393220
  15.5 11.3 %copy-start.7 = (f32[2,128,128]{2,1,0:T(8,128)S(1)}, f32[2,128,128]{2,1,0:T(8,128)}, u32[]{:S(2)}) copy-start(f32[2,128,128]{2,1,0:T(8,128)} %get-tuple-element.84.sine_ref) | copy-start | bytes 393220
  15.6 11.3 %copy-start.8 = (f32[2,128,128]{2,1,0:T(8,128)S(1)}, f32[2,128,128]{2,1,0:T(8,128)}, u32[]{:S(2)}) copy-start(f32[2,128,128]{2,1,0:T(8,128)} %get-tuple-element.85.cosine_ref) | copy-start | bytes 393220
  22.6 81.1 %collective-permute-start.6 = (bf16[4096,128]{1,0:T(8,128)(2,1)}, bf16[4096,128]{1,0:T(8,128)(2,1)S(1)}, u32[]{:S(2)}, u32[]{:S(2)}) collective-permute-start(bf16[4096,128]{1,0:T(8,128)(2,1)} %get-tuple-element.46), channel_id=1, source_target_pairs={{0,2},{2,0},{4,6},{6,4},{8,10},{10,8},{12,14},{14,12},{1,3},{3,1},... | collective-permute-start | bytes 3145736 | tf_op jit(solution)/shard_map/ppermute | solution.py:683
  24.6 83.0 %collective-permute-start.7 = (bf16[4096,128]{1,0:T(8,128)(2,1)}, bf16[4096,128]{1,0:T(8,128)(2,1)S(1)}, u32[]{:S(2)}, u32[]{:S(2)}) collective-permute-start(bf16[4096,128]{1,0:T(8,128)(2,1)} %get-tuple-element.47), channel_id=1, source_target_pairs={{0,4},{2,6},{4,0},{6,2},{8,12},{10,14},{12,8},{14,10},{1,5},{3,7},... | collective-permute-start | bytes 3145736 | tf_op jit(solution)/shard_map/ppermute | solution.py:683
  26.1 104.5 %collective-permute-start.8 = (bf16[4096,128]{1,0:T(8,128)(2,1)}, bf16[4096,128]{1,0:T(8,128)(2,1)S(1)}, u32[]{:S(2)}, u32[]{:S(2)}) collective-permute-start(bf16[4096,128]{1,0:T(8,128)(2,1)} %get-tuple-element.48), channel_id=1, source_target_pairs={{0,6},{2,4},{4,2},{6,0},{8,14},{10,12},{12,10},{14,8},{1,7},{3,5},... | collective-permute-start | bytes 3145736 | tf_op jit(solution)/shard_map/ppermute | solution.py:683
  28.3 11.2 %copy-start.21 = (bf16[1,128,4,128]{3,2,1,0:T(4,128)(2,1)S(1)}, bf16[1,128,4,128]{3,2,1,0:T(4,128)(2,1)}, u32[]{:S(2)}) copy-start(bf16[1,128,4,128]{3,2,1,0:T(4,128)(2,1)} %param.15) | copy-start | bytes 393220
  28.3 11.2 %copy-start.20 = (bf16[1,128,4,128]{3,2,1,0:T(4,128)(2,1)S(1)}, bf16[1,128,4,128]{3,2,1,0:T(4,128)(2,1)}, u32[]{:S(2)}) copy-start(bf16[1,128,4,128]{3,2,1,0:T(4,128)(2,1)} %param.13) | copy-start | bytes 393220
  28.3 11.9 %copy-start.23 = (bf16[1,128,4,128]{3,2,1,0:T(4,128)(2,1)S(1)}, bf16[1,128,4,128]{3,2,1,0:T(4,128)(2,1)}, u32[]{:S(2)}) copy-start(bf16[1,128,4,128]{3,2,1,0:T(4,128)(2,1)} %param.16) | copy-start | bytes 393220
  36.0 61.1 %collective-permute-start.3 = (bf16[2304,128]{1,0:T(8,128)(2,1)}, bf16[2304,128]{1,0:T(8,128)(2,1)S(1)}, u32[]{:S(2)}, u32[]{:S(2)}) collective-permute-start(bf16[2304,128]{1,0:T(8,128)(2,1)} %get-tuple-element.43), channel_id=1, source_target_pairs={{0,2},{2,0},{4,6},{6,4},{8,10},{10,8},{12,14},{14,12},{1,3},{3,1},... | collective-permute-start | bytes 1769480 | tf_op jit(solution)/shard_map/ppermute | solution.py:683
  37.9 104.9 %collective-permute-start.4 = (bf16[2304,128]{1,0:T(8,128)(2,1)}, bf16[2304,128]{1,0:T(8,128)(2,1)}, u32[]{:S(2)}, u32[]{:S(2)}) collective-permute-start(bf16[2304,128]{1,0:T(8,128)(2,1)} %get-tuple-element.44), channel_id=1, source_target_pairs={{0,4},{2,6},{4,0},{6,2},{8,12},{10,14},{12,8},{14,10},{1,5},{3,7},... | collective-permute-start | bytes 1769480 | tf_op jit(solution)/shard_map/ppermute | solution.py:683
  97.0 33.5 %copy-start.6 = (bf16[2304,128]{1,0:T(8,128)(2,1)}, bf16[2304,128]{1,0:T(8,128)(2,1)S(1)}, u32[]{:S(2)}) copy-start(bf16[2304,128]{1,0:T(8,128)(2,1)S(1)} %collective-permute-done.3.refs_1_) | copy-start | bytes 1769476
  97.0 64.7 %collective-permute-start.5 = (bf16[2304,128]{1,0:T(8,128)(2,1)}, bf16[2304,128]{1,0:T(8,128)(2,1)}, u32[]{:S(2)}, u32[]{:S(2)}) collective-permute-start(bf16[2304,128]{1,0:T(8,128)(2,1)} %get-tuple-element.45), channel_id=1, source_target_pairs={{0,6},{2,4},{4,2},{6,0},{8,14},{10,12},{12,10},{14,8},{1,7},{3,5},... | collective-permute-start | bytes 1769480 | tf_op jit(solution)/shard_map/ppermute | solution.py:683
  103.7 28.3 %copy-start = (bf16[4096,128]{1,0:T(8,128)(2,1)}, bf16[4096,128]{1,0:T(8,128)(2,1)S(1)}, u32[]{:S(2)}) copy-start(bf16[4096,128]{1,0:T(8,128)(2,1)S(1)} %collective-permute-done.6.refs_1_.refs_9_) | copy-start | bytes 3145732
  103.7 67.8 %collective-permute-start = (bf16[2048,128]{1,0:T(8,128)(2,1)}, bf16[2048,128]{1,0:T(8,128)(2,1)}, u32[]{:S(2)}, u32[]{:S(2)}) collective-permute-start(bf16[2048,128]{1,0:T(8,128)(2,1)} %get-tuple-element.39), channel_id=1, source_target_pairs={{0,2},{2,0},{4,6},{6,4},{8,10},{10,8},{12,14},{14,12},{1,3},{3,1},... | collective-permute-start | bytes 1572872 | tf_op jit(solution)/shard_map/ppermute | solution.py:683
  107.5 24.5 %copy-start.1 = (bf16[4096,128]{1,0:T(8,128)(2,1)}, bf16[4096,128]{1,0:T(8,128)(2,1)S(1)}, u32[]{:S(2)}) copy-start(bf16[4096,128]{1,0:T(8,128)(2,1)S(1)} %collective-permute-done.7.refs_2_.refs_10_) | copy-start | bytes 3145732
  107.5 70.7 %collective-permute-start.1 = (bf16[2048,128]{1,0:T(8,128)(2,1)}, bf16[2048,128]{1,0:T(8,128)(2,1)}, u32[]{:S(2)}, u32[]{:S(2)}) collective-permute-start(bf16[2048,128]{1,0:T(8,128)(2,1)} %get-tuple-element.40), channel_id=1, source_target_pairs={{0,4},{2,6},{4,0},{6,2},{8,12},{10,14},{12,8},{14,10},{1,5},{3,7},... | collective-permute-start | bytes 1572872 | tf_op jit(solution)/shard_map/ppermute | solution.py:683
  130.6 1.5 copy-start.2
  130.6 58.4 %collective-permute-start.2 = (bf16[2048,128]{1,0:T(8,128)(2,1)}, bf16[2048,128]{1,0:T(8,128)(2,1)}, u32[]{:S(2)}, u32[]{:S(2)}) collective-permute-start(bf16[2048,128]{1,0:T(8,128)(2,1)} %get-tuple-element.41), channel_id=1, source_target_pairs={{0,6},{2,4},{4,2},{6,0},{8,14},{10,12},{12,10},{14,8},{1,7},{3,5},... | collective-permute-start | bytes 1572872 | tf_op jit(solution)/shard_map/ppermute | solution.py:683
  142.8 46.2 %collective-permute-start.9 = (bf16[1056,128]{1,0:T(8,128)(2,1)}, bf16[1056,128]{1,0:T(8,128)(2,1)S(1)}, u32[]{:S(2)}, u32[]{:S(2)}) collective-permute-start(bf16[1056,128]{1,0:T(8,128)(2,1)} %get-tuple-element.53), channel_id=1, source_target_pairs={{0,8},{2,10},{4,12},{6,14},{8,0},{10,2},{12,4},{14,6},{1,9},{3,11}... | collective-permute-start | bytes 811016 | tf_op jit(solution)/shard_map/ppermute | solution.py:683
  157.4 14.1 %copy-start.26 = (bf16[1056,128]{1,0:T(8,128)(2,1)S(1)}, bf16[1056,128]{1,0:T(8,128)(2,1)}, u32[]{:S(2)}) copy-start(bf16[1056,128]{1,0:T(8,128)(2,1)} %get-tuple-element.55) | copy-start | bytes 811012
  157.4 20.8 %copy-start.25 = (bf16[1056,128]{1,0:T(8,128)(2,1)S(1)}, bf16[1056,128]{1,0:T(8,128)(2,1)}, u32[]{:S(2)}) copy-start(bf16[1056,128]{1,0:T(8,128)(2,1)} %get-tuple-element.56) | copy-start | bytes 811012
  161.8 47.3 %collective-permute-start.10 = (bf16[1056,128]{1,0:T(8,128)(2,1)}, bf16[1056,128]{1,0:T(8,128)(2,1)S(1)}, u32[]{:S(2)}, u32[]{:S(2)}) collective-permute-start(bf16[1056,128]{1,0:T(8,128)(2,1)} %get-tuple-element.54), channel_id=1, source_target_pairs={{0,10},{2,8},{4,14},{6,12},{8,2},{10,0},{12,6},{14,4},{1,11},{3,9}... | collective-permute-start | bytes 811016 | tf_op jit(solution)/shard_map/ppermute | solution.py:683
  171.5 39.2 %collective-permute-start.11 = (bf16[1056,128]{1,0:T(8,128)(2,1)S(1)}, bf16[1056,128]{1,0:T(8,128)(2,1)S(1)}, u32[]{:S(2)}, u32[]{:S(2)}) collective-permute-start(bf16[1056,128]{1,0:T(8,128)(2,1)S(1)} %copy-done.26), channel_id=1, source_target_pairs={{0,12},{2,14},{4,8},{6,10},{8,4},{10,6},{12,0},{14,2},{1,13},{3,15... | collective-permute-start | bytes 811016 | tf_op jit(solution)/shard_map/ppermute | solution.py:683
  178.3 34.7 %collective-permute-start.12 = (bf16[1056,128]{1,0:T(8,128)(2,1)S(1)}, bf16[1056,128]{1,0:T(8,128)(2,1)S(1)}, u32[]{:S(2)}, u32[]{:S(2)}) collective-permute-start(bf16[1056,128]{1,0:T(8,128)(2,1)S(1)} %copy-done.25), channel_id=1, source_target_pairs={{0,14},{2,12},{4,10},{6,8},{8,6},{10,4},{12,2},{14,0},{1,15},{3,13... | collective-permute-start | bytes 811016 | tf_op jit(solution)/shard_map/ppermute | solution.py:683
  189.0 27.1 %collective-permute-start.13 = (bf16[1056,128]{1,0:T(8,128)(2,1)}, bf16[1056,128]{1,0:T(8,128)(2,1)S(1)}, u32[]{:S(2)}, u32[]{:S(2)}) collective-permute-start(bf16[1056,128]{1,0:T(8,128)(2,1)} %get-tuple-element.57), channel_id=1, source_target_pairs={{0,4},{2,6},{4,0},{6,2},{8,12},{10,14},{12,8},{14,10},{1,5},{3,7},... | collective-permute-start | bytes 811016 | tf_op jit(solution)/shard_map/ppermute | solution.py:683
  189.0 20.1 %copy-start.9 = (bf16[1056,128]{1,0:T(8,128)(2,1)}, bf16[1056,128]{1,0:T(8,128)(2,1)S(1)}, u32[]{:S(2)}) copy-start(bf16[1056,128]{1,0:T(8,128)(2,1)S(1)} %collective-permute-done.9.refs_5_.refs_4_.refs_13_) | copy-start | bytes 811012
  189.0 27.8 %collective-permute-start.14 = (bf16[1056,128]{1,0:T(8,128)(2,1)}, bf16[1056,128]{1,0:T(8,128)(2,1)S(1)}, u32[]{:S(2)}, u32[]{:S(2)}) collective-permute-start(bf16[1056,128]{1,0:T(8,128)(2,1)} %get-tuple-element.58), channel_id=1, source_target_pairs={{0,6},{2,4},{4,2},{6,0},{8,14},{10,12},{12,10},{14,8},{1,7},{3,5},... | collective-permute-start | bytes 811016 | tf_op jit(solution)/shard_map/ppermute | solution.py:683
  209.1 7.7 %copy-start.10 = (bf16[1056,128]{1,0:T(8,128)(2,1)}, bf16[1056,128]{1,0:T(8,128)(2,1)S(1)}, u32[]{:S(2)}) copy-start(bf16[1056,128]{1,0:T(8,128)(2,1)S(1)} %collective-permute-done.10.refs_6_.refs_5_.refs_14_) | copy-start | bytes 811012
  209.1 33.5 %collective-permute-start.16 = (bf16[1056,128]{1,0:T(8,128)(2,1)}, bf16[1056,128]{1,0:T(8,128)(2,1)S(1)}, u32[]{:S(2)}, u32[]{:S(2)}) collective-permute-start(bf16[1056,128]{1,0:T(8,128)(2,1)} %get-tuple-element.64), channel_id=1, source_target_pairs={{0,8},{2,10},{4,12},{6,14},{8,0},{10,2},{12,4},{14,6},{1,9},{3,11}... | collective-permute-start | bytes 811016 | tf_op jit(solution)/shard_map/ppermute | solution.py:683
  210.8 6.1 %copy-start.11 = (bf16[1056,128]{1,0:T(8,128)(2,1)}, bf16[1056,128]{1,0:T(8,128)(2,1)S(1)}, u32[]{:S(2)}) copy-start(bf16[1056,128]{1,0:T(8,128)(2,1)S(1)} %collective-permute-done.11.refs_7_.refs_6_.refs_15_) | copy-start | bytes 811012
  210.8 38.3 %collective-permute-start.17 = (bf16[1056,128]{1,0:T(8,128)(2,1)}, bf16[1056,128]{1,0:T(8,128)(2,1)S(1)}, u32[]{:S(2)}, u32[]{:S(2)}) collective-permute-start(bf16[1056,128]{1,0:T(8,128)(2,1)} %get-tuple-element.65), channel_id=1, source_target_pairs={{0,10},{2,8},{4,14},{6,12},{8,2},{10,0},{12,6},{14,4},{1,11},{3,9}... | collective-permute-start | bytes 811016 | tf_op jit(solution)/shard_map/ppermute | solution.py:683
  213.0 3.8 %copy-start.12 = (bf16[1056,128]{1,0:T(8,128)(2,1)}, bf16[1056,128]{1,0:T(8,128)(2,1)S(1)}, u32[]{:S(2)}) copy-start(bf16[1056,128]{1,0:T(8,128)(2,1)S(1)} %collective-permute-done.12.refs_8_.refs_7_.refs_16_) | copy-start | bytes 811012
  213.0 36.0 %collective-permute-start.18 = (bf16[1056,128]{1,0:T(8,128)(2,1)}, bf16[1056,128]{1,0:T(8,128)(2,1)S(1)}, u32[]{:S(2)}, u32[]{:S(2)}) collective-permute-start(bf16[1056,128]{1,0:T(8,128)(2,1)} %get-tuple-element.66), channel_id=1, source_target_pairs={{0,12},{2,14},{4,8},{6,10},{8,4},{10,6},{12,0},{14,2},{1,13},{3,15... | collective-permute-start | bytes 811016 | tf_op jit(solution)/shard_map/ppermute | solution.py:683
  216.0 0.8 copy-start.13
  216.0 52.4 %collective-permute-start.22 = (bf16[1056,128]{1,0:T(8,128)(2,1)}, bf16[1056,128]{1,0:T(8,128)(2,1)S(1)}, u32[]{:S(2)}, u32[]{:S(2)}) collective-permute-start(bf16[1056,128]{1,0:T(8,128)(2,1)} %get-tuple-element.71), channel_id=1, source_target_pairs={{0,14},{2,12},{4,10},{6,8},{8,6},{10,4},{12,2},{14,0},{1,15},{3,13... | collective-permute-start | bytes 811016 | tf_op jit(solution)/shard_map/ppermute | solution.py:683
  226.4 36.1 %collective-permute-start.15 = (bf16[1056,128]{1,0:T(8,128)(2,1)}, bf16[1056,128]{1,0:T(8,128)(2,1)S(1)}, u32[]{:S(2)}, u32[]{:S(2)}) collective-permute-start(bf16[1056,128]{1,0:T(8,128)(2,1)} %get-tuple-element.60), channel_id=1, source_target_pairs={{0,2},{2,0},{4,6},{6,4},{8,10},{10,8},{12,14},{14,12},{1,3},{3,1},... | collective-permute-start | bytes 811016 | tf_op jit(solution)/shard_map/ppermute | solution.py:683
  242.6 19.9 %copy-start.3 = (bf16[1056,128]{1,0:T(8,128)(2,1)}, bf16[1056,128]{1,0:T(8,128)(2,1)S(1)}, u32[]{:S(2)}) copy-start(bf16[1056,128]{1,0:T(8,128)(2,1)S(1)} %collective-permute-done.16.refs_19_.refs_4_.refs_13_) | copy-start | bytes 811012
  242.6 25.9 %collective-permute-start.19 = (bf16[1056,128]{1,0:T(8,128)(2,1)}, bf16[1056,128]{1,0:T(8,128)(2,1)S(1)}, u32[]{:S(2)}, u32[]{:S(2)}) collective-permute-start(bf16[1056,128]{1,0:T(8,128)(2,1)} %get-tuple-element.68), channel_id=1, source_target_pairs={{0,2},{2,0},{4,6},{6,4},{8,10},{10,8},{12,14},{14,12},{1,3},{3,1},... | collective-permute-start | bytes 811016 | tf_op jit(solution)/shard_map/ppermute | solution.py:683
  249.0 13.5 %copy-start.4 = (bf16[1056,128]{1,0:T(8,128)(2,1)}, bf16[1056,128]{1,0:T(8,128)(2,1)S(1)}, u32[]{:S(2)}) copy-start(bf16[1056,128]{1,0:T(8,128)(2,1)S(1)} %collective-permute-done.17.refs_20_.refs_5_.refs_14_) | copy-start | bytes 811012
  249.0 19.5 %collective-permute-start.20 = (bf16[1056,128]{1,0:T(8,128)(2,1)}, bf16[1056,128]{1,0:T(8,128)(2,1)S(1)}, u32[]{:S(2)}, u32[]{:S(2)}) collective-permute-start(bf16[1056,128]{1,0:T(8,128)(2,1)} %get-tuple-element.69), channel_id=1, source_target_pairs={{0,4},{2,6},{4,0},{6,2},{8,12},{10,14},{12,8},{14,10},{1,5},{3,7},... | collective-permute-start | bytes 811016 | tf_op jit(solution)/shard_map/ppermute | solution.py:683
  249.0 13.5 %copy-start.5 = (bf16[1056,128]{1,0:T(8,128)(2,1)}, bf16[1056,128]{1,0:T(8,128)(2,1)S(1)}, u32[]{:S(2)}) copy-start(bf16[1056,128]{1,0:T(8,128)(2,1)S(1)} %collective-permute-done.18.refs_21_.refs_6_.refs_15_) | copy-start | bytes 811012
  249.0 19.5 %collective-permute-start.21 = (bf16[1056,128]{1,0:T(8,128)(2,1)}, bf16[1056,128]{1,0:T(8,128)(2,1)S(1)}, u32[]{:S(2)}, u32[]{:S(2)}) collective-permute-start(bf16[1056,128]{1,0:T(8,128)(2,1)} %get-tuple-element.70), channel_id=1, source_target_pairs={{0,6},{2,4},{4,2},{6,0},{8,14},{10,12},{12,10},{14,8},{1,7},{3,5},... | collective-permute-start | bytes 811016 | tf_op jit(solution)/shard_map/ppermute | solution.py:683
  268.5 0.8 copy-start.17
  268.5 0.8 copy-start.18
  268.5 0.9 copy-start.19
  (3 other events, 2.2 us)
where the time goes:
time: 276 us; the launch traced here: 275 us
  Pallas kernels  115 us (42%)
  waiting for transfers between devices  102 us (37%)
  starting transfers between devices  45.7 us (17%)
  other arithmetic  5.97 us (2%)
  local copies, waits for them, and re-layouts  5.34 us (2%)
    ppermute x23, waiting for transfers between devices, swap(): lax.ppermute(array, 'node', [(node, node ^ apart) for node in range(peer_...  102 us
    pallas_call x3, Pallas kernels, attend_second(): pl.pallas_call(functools.partial(second_kernel, head_count, len(far), tas...  39.7 us
    ppermute x23, starting transfers between devices, swap(): lax.ppermute(array, 'node', [(node, node ^ apart) for node in range(peer_...  38.3 us
    pallas_call x4, Pallas kernels, attend_first(): pl.pallas_call(functools.partial(first_kernel, len(sources), task_count,...  35.8 us
    pallas_call x2, Pallas kernels, pack(): pl.pallas_call(functools.partial(pack_kernel, per_peer, head_count, token...  14.7 us
    pallas_call x2, Pallas kernels, merge(): pl.pallas_call(functools.partial(merge_kernel, head_count, group_size, le...  10.4 us
    pallas_call x2, Pallas kernels, attend_own(): pl.pallas_call(functools.partial(own_kernel, row_count // token_count, sc...  10.4 us
    all_to_all x1, starting transfers between devices, local(): got = lax.all_to_all(send, 'node', split_axis=0, concat_axis=0, tiled=True)  7.41 us
  transfers between devices with their start and end apart: 24, of which 9 were waited for; matrix products, arithmetic and copies ran while one was open for 3% of the time, Pallas kernels for 38%

commit v1 on v0

--- a/solution.py
+++ b/solution.py
@@ -794,17 +794,13 @@
             list(range(base, base + head_count)), lambda step: base + step, before
         )
         before = (*before, *parts_one[base : base + head_count])
+    before = second(list(range(1, head_count)), lambda step: step + 1, before)
     before = first(
         nearer,
         list(range(1, half)) + [0],
         lambda step: (step + 1) % half,
         lambda task, place: task,
         (*before, *parts_one[half:head_count]),
-    )
-    before = second(
-        list(range(1, head_count)),
-        lambda step: step + 1,
-        before,
     )
     before = second([0], lambda step: 0, before)
     before = (*before, *parts_two[head_count : head_count + 3])

time: 276 us -> 276 us (level)
  waiting for transfers between devices: 102 us -> 96.8 us
  starting transfers between devices: 45.7 us -> 50.6 us
    ppermute x23, waiting for transfers between devices: 102 us -> 96.8 us  [swap(): lax.ppermute(array, 'node', [(node, node ^ apart) for node in range(peer_...]
    ppermute x23, starting transfers between devices: 38.3 us -> 43.2 us  [swap(): lax.ppermute(array, 'node', [(node, node ^ apart) for node in range(peer_...]
  transfers between devices with their start and end apart: 24 -> 24, of which waited for: 9 -> 7; matrix products, arithmetic and copies ran while one was open for 3% -> 3% of each run, Pallas kernels for 38% -> 39%
where the time goes in v1:
time: 276 us; the launch traced here: 275 us
  Pallas kernels  115 us (42%)
  waiting for transfers between devices  96.8 us (35%)
  starting transfers between devices  50.6 us (18%)
  other arithmetic  6.01 us (2%)
  local copies, waits for them, and re-layouts  5.43 us (2%)
    ppermute x23, waiting for transfers between devices, swap(): lax.ppermute(array, 'node', [(node, node ^ apart) for node in range(peer_...  96.8 us
    ppermute x23, starting transfers between devices, swap(): lax.ppermute(array, 'node', [(node, node ^ apart) for node in range(peer_...  43.2 us
    pallas_call x3, Pallas kernels, attend_second(): pl.pallas_call(functools.partial(second_kernel, head_count, len(far), tas...  39.7 us
    pallas_call x4, Pallas kernels, attend_first(): pl.pallas_call(functools.partial(first_kernel, len(sources), task_count,...  36 us
    pallas_call x2, Pallas kernels, pack(): pl.pallas_call(functools.partial(pack_kernel, per_peer, head_count, token...  14.7 us
    pallas_call x2, Pallas kernels, merge(): pl.pallas_call(functools.partial(merge_kernel, head_count, group_size, le...  10.4 us
    pallas_call x2, Pallas kernels, attend_own(): pl.pallas_call(functools.partial(own_kernel, row_count // token_count, sc...  10.4 us
    all_to_all x1, starting transfers between devices, local(): got = lax.all_to_all(send, 'node', split_axis=0, concat_axis=0, tiled=True)  7.41 us
  transfers between devices with their start and end apart: 24, of which 7 were waited for; matrix products, arithmetic and copies ran while one was open for 3% of the time, Pallas kernels for 39%

profile of v1, /device:TPU:0, one launch (start us, length us, event | category | flops | bytes accessed | tf_op | source)
XLA Modules:
  0.0 275.1 jit_solution(1711350691831087802)
XLA Ops:
  0.7 0.7 convert_element_type.47
  1.3 1.3 fusion.6
  2.6 3.8 %turn_queries.1.refs_8_.query_ref = bf16[8,2,1024,128]{3,2,1,0:T(8,128)(2,1)} custom-call(bf16[1,128,32,128]{3,2,1,0:T(8,128)(2,1)} %first_ref.1, bf16[1,128,32,128]{3,2,1,0:T(8,128)(2,1)} %second_ref.1, f32[2,128,128]{2,1,0:T(8,128)} %get-tuple-element.85.cosine_ref, f32[2,128,128]{2,1,0:T(8,128)} %get-tuple-element.84.sine_ref), custom_call_target="tpu_custom_call" | custom-call | flops 4194304 | bytes 6291456 | tf_op jit(solution)/shard_map/turn_queries/pallas_call | solution.py:55
  6.4 7.4 %all-to-all-start = ((bf16[8,2,1024,128]{3,2,1,0:T(8,128)(2,1)}), bf16[8,2,1024,128]{3,2,1,0:T(8,128)(2,1)}, u32[]{:S(2)}, u32[]{:S(2)}) async-start(bf16[8,2,1024,128]{3,2,1,0:T(8,128)(2,1)} %turn_queries.1.refs_8_.query_ref), calls=%async_computation | async-start | bytes 8388608 | tf_op jit(solution)/shard_map/all_to_all | solution.py:687
  15.5 7.1 %pack_rows.2 = (bf16[4096,128]{1,0:T(8,128)(2,1)}, bf16[4096,128]{1,0:T(8,128)(2,1)}, bf16[4096,128]{1,0:T(8,128)(2,1)}, bf16[4096,128]{1,0:T(8,128)(2,1)}) custom-call(s32[32]{0:T(128)} %reshape.65.index_ref, s32[3]{0:T(128)} %add_add_fusion.1.place_ref, bf16[32,512,128]{2,1,0:T(8,128)(2,1)} %bitcast.44, bf16[32,512,128]{2,1,0:T(8,128)(2,1)} %bitcast.45, ...), custom_call_target="tpu_custom_call" | custom-call | bytes 8388608 | tf_op jit(solution)/shard_map/pack_rows/pallas_call | solution.py:163
  22.6 2.0 collective-permute-start.6
  24.6 1.4 collective-permute-start.7
  27.0 0.8 fusion.1.refs_8_
  28.4 7.7 %pack_rows.3 = (bf16[2304,128]{1,0:T(8,128)(2,1)}, bf16[2304,128]{1,0:T(8,128)(2,1)}, bf16[2304,128]{1,0:T(8,128)(2,1)}, bf16[2304,128]{1,0:T(8,128)(2,1)}, bf16...) custom-call(s32[32]{0:T(128)} %reshape.65.index_ref, ...), custom_call_target="tpu_custom_call" | custom-call | bytes 4718592 | tf_op jit(solution)/shard_map/pack_rows/pallas_call | solution.py:163
  36.1 2.0 collective-permute-start.3
  38.1 1.3 collective-permute-start.4
  39.4 0.7 copy.49
  40.1 0.7 copy.48
  40.9 0.8 fusion.7.key_ref
  41.7 5.2 %attend_own.3.refs_5_.refs_8_.refs_17_ = bf16[4,1056,128]{2,1,0:T(8,128)(2,1)} custom-call(s32[3]{0:T(128)} %add_add_fusion.place_ref, bf16[8,2,1024,128]{3,2,1,0:T(8,128)(2,1)} %turn_queries.1.refs_8_.query_ref, bf16[4,128,128]{2,1,0:T(8,128)(2,1)} %fusion.7.key_ref, bf16[4,128,128]{2,1,0:T(8,128)(2,1)} %bitcast.67), custom_call_target="tpu_custom_call" | custom-call | flops 268435456 | bytes 2359296 | tf_op jit(solution)/shard_map/attend_own/pallas_call | solution.py:533
  46.9 50.1 %collective-permute-done.3.refs_1_ = bf16[2304,128]{1,0:T(8,128)(2,1)S(1)} collective-permute-done((bf16[2304,128]{1,0:T(8,128)(2,1)}, bf16[2304,128]{1,0:T(8,128)(2,1)S(1)}, u32[]{:S(2)}, u32[]{:S(2)}) %collective-permute-start.3) | collective-permute-done | bytes 589856 | tf_op jit(solution)/shard_map/ppermute | solution.py:683
  97.0 0.6 collective-permute-start.5
  97.7 0.8 fusion.8.key_ref
  98.5 5.2 %attend_own.2.refs_4_.refs_8_.refs_17_ = bf16[4,1056,128]{2,1,0:T(8,128)(2,1)} custom-call(s32[3]{0:T(128)} %add_add_fusion.place_ref, bf16[8,2,1024,128]{3,2,1,0:T(8,128)(2,1)} %turn_queries.1.refs_8_.query_ref, bf16[4,128,128]{2,1,0:T(8,128)(2,1)} %fusion.8.key_ref, bf16[4,128,128]{2,1,0:T(8,128)(2,1)} %bitcast.66), custom_call_target="tpu_custom_call" | custom-call | flops 268435456 | bytes 2359296 | tf_op jit(solution)/shard_map/attend_own/pallas_call | solution.py:533
  103.7 0.9 collective-permute-start
  104.6 2.9 %collective-permute-done.7.refs_2_.refs_10_ = bf16[4096,128]{1,0:T(8,128)(2,1)S(1)} collective-permute-done((bf16[4096,128]{1,0:T(8,128)(2,1)}, bf16[4096,128]{1,0:T(8,128)(2,1)S(1)}, u32[]{:S(2)}, u32[]{:S(2)}) %collective-permute-start.7) | collective-permute-done | bytes 1048608 | tf_op jit(solution)/shard_map/ppermute | solution.py:683
  107.5 1.1 collective-permute-start.1
  108.6 22.0 %collective-permute-done.8.refs_3_.refs_11_ = bf16[4096,128]{1,0:T(8,128)(2,1)S(1)} collective-permute-done((bf16[4096,128]{1,0:T(8,128)(2,1)}, bf16[4096,128]{1,0:T(8,128)(2,1)S(1)}, u32[]{:S(2)}, u32[]{:S(2)}) %collective-permute-start.8) | collective-permute-done | bytes 1048608 | tf_op jit(solution)/shard_map/ppermute | solution.py:683
  130.6 1.4 collective-permute-start.2
  132.0 5.7 %attend_first.4 = (bf16[1056,128]{1,0:T(8,128)(2,1)}, f32[8,128]{1,0:T(8,128)}) custom-call(s32[3]{0:T(128)} %add_add_fusion.place_ref, bf16[8,2,1024,128]{3,2,1,0:T(8,128)(2,1)} %all-to-all-done.query_ref, bf16[4096,128]{1,0:T(8,128)(2,1)} %get-tuple-element.37.refs_10_.refs_0_.refs_8_, bf16[4096,128]{1,0:T(8,128)(2,1)} %copy-done, ...), custom_call_target="tpu_custom_call" | custom-call | flops 1073741824 | bytes 1572864 | tf_op jit(solution)/shard_map/attend_first/pallas_call | solution.py:324
  137.8 12.2 %attend_first.5 = (bf16[1056,128]{1,0:T(8,128)(2,1)}, bf16[1056,128]{1,0:T(8,128)(2,1)}, bf16[1056,128]{1,0:T(8,128)(2,1)}, f32[8,128]{1,0:T(8,128)}) custom-call(s32[3]{0:T(128)} %add_add_fusion.place_ref, bf16[8,2,1024,128]{3,2,1,0:T(8,128)(2,1)} %all-to-all-done.query_ref, bf16[4096,128]{1,0:T(8,128)(2,1)} %get-tuple-element.37.refs_10_.refs_0_.refs_8_, ...), custom_call_target="tpu_custom_call" | custom-call | flops 3221225472 | bytes 4718592 | tf_op jit(solution)/shard_map/attend_first/pallas_call | solution.py:324
  150.0 2.5 collective-permute-start.9
  152.5 9.2 %collective-permute-done.5.refs_3_ = bf16[2304,128]{1,0:T(8,128)(2,1)} collective-permute-done((bf16[2304,128]{1,0:T(8,128)(2,1)}, bf16[2304,128]{1,0:T(8,128)(2,1)}, u32[]{:S(2)}, u32[]{:S(2)}) %collective-permute-start.5) | collective-permute-done | bytes 589856 | tf_op jit(solution)/shard_map/ppermute | solution.py:683
  161.7 0.8 collective-permute-start.10
  162.5 9.0 %attend_first.6 = (bf16[1056,128]{1,0:T(8,128)(2,1)}, bf16[1056,128]{1,0:T(8,128)(2,1)}, f32[8,128]{1,0:T(8,128)}) custom-call(s32[3]{0:T(128)} %add_add_fusion.place_ref, bf16[8,2,1024,128]{3,2,1,0:T(8,128)(2,1)} %all-to-all-done.query_ref, bf16[2304,128]{1,0:T(8,128)(2,1)} %get-tuple-element.42.refs_0_, bf16[2304,128]{1,0:T(8,128)(2,1)} %copy-done.10, ...), custom_call_target="tpu_custom_call" | custom-call | flops 2147483648 | bytes 3145728 | tf_op jit(solution)/shard_map/attend_first/pallas_call | solution.py:324
  171.5 2.0 collective-permute-start.11
  173.5 4.7 %collective-permute-done.1.refs_6_.refs_2_ = bf16[2048,128]{1,0:T(8,128)(2,1)} collective-permute-done((bf16[2048,128]{1,0:T(8,128)(2,1)}, bf16[2048,128]{1,0:T(8,128)(2,1)}, u32[]{:S(2)}, u32[]{:S(2)}) %collective-permute-start.1) | collective-permute-done | bytes 524320 | tf_op jit(solution)/shard_map/ppermute | solution.py:683
  178.2 3.2 %collective-permute-start.12 = (bf16[1056,128]{1,0:T(8,128)(2,1)S(1)}, bf16[1056,128]{1,0:T(8,128)(2,1)S(1)}, u32[]{:S(2)}, u32[]{:S(2)}) collective-permute-start(bf16[1056,128]{1,0:T(8,128)(2,1)S(1)} %copy-done.29), channel_id=1, source_target_pairs={{0,14},{2,12},{4,10},{6,8},{8,6},{10,4},{12,2},{14,0},{1,15},{3,13... | collective-permute-start | bytes 811016 | tf_op jit(solution)/shard_map/ppermute | solution.py:683
  181.4 7.5 %collective-permute-done.2.refs_7_.refs_3_ = bf16[2048,128]{1,0:T(8,128)(2,1)} collective-permute-done((bf16[2048,128]{1,0:T(8,128)(2,1)}, bf16[2048,128]{1,0:T(8,128)(2,1)}, u32[]{:S(2)}, u32[]{:S(2)}) %collective-permute-start.2) | collective-permute-done | bytes 524320 | tf_op jit(solution)/shard_map/ppermute | solution.py:683
  189.0 18.2 %attend_second.3 = (bf16[1056,128]{1,0:T(8,128)(2,1)}, bf16[1056,128]{1,0:T(8,128)(2,1)}, bf16[1056,128]{1,0:T(8,128)(2,1)}, bf16[1056,128]{1,0:T(8,128)(2,1)}, f32[8,128]{1,0:T(8,128)}) custom-call(s32[8]{0:T(128)} %parent_ref.5, s32[3]{0:T(128)} %add_add_fusion.place_ref, bf16[8,2,1024,128]{3,2,1,0:T(8,128)(2,1)} %all-to-all-done.query_ref, ...), custom_call_target="tpu_custom_call" | custom-call | flops 4563402752 | bytes 6553600 | tf_op jit(solution)/shard_map/attend_second/pallas_call | solution.py:465
  207.2 2.0 collective-permute-start.14
  209.2 1.7 collective-permute-start.16
  210.9 2.1 collective-permute-start.17
  213.1 3.1 %collective-permute-start.18 = (bf16[1056,128]{1,0:T(8,128)(2,1)}, bf16[1056,128]{1,0:T(8,128)(2,1)S(1)}, u32[]{:S(2)}, u32[]{:S(2)}) collective-permute-start(bf16[1056,128]{1,0:T(8,128)(2,1)} %get-tuple-element.66), channel_id=1, source_target_pairs={{0,12},{2,14},{4,8},{6,10},{8,4},{10,6},{12,0},{14,2},{1,13},{3,15... | collective-permute-start | bytes 811016 | tf_op jit(solution)/shard_map/ppermute | solution.py:683
  216.2 14.4 %attend_second.4 = (bf16[1056,128]{1,0:T(8,128)(2,1)}, bf16[1056,128]{1,0:T(8,128)(2,1)}, bf16[1056,128]{1,0:T(8,128)(2,1)}, f32[8,128]{1,0:T(8,128)}) custom-call(s32[8]{0:T(128)} %parent_ref.5, s32[3]{0:T(128)} %add_add_fusion.place_ref, bf16[8,2,1024,128]{3,2,1,0:T(8,128)(2,1)} %all-to-all-done.query_ref, bf16[2304,128]{1,0:T(8,128)(2,1)} %get-tuple-element.42.refs_0_, ...), custom_call_target="tpu_custom_call" | custom-call | flops 3422552064 | bytes 4915200 | tf_op jit(solution)/shard_map/attend_second/pallas_call | solution.py:465
  230.6 0.7 copy-done.13
  231.4 9.1 %attend_first.7 = (bf16[1056,128]{1,0:T(8,128)(2,1)}, bf16[1056,128]{1,0:T(8,128)(2,1)}, f32[8,128]{1,0:T(8,128)}) custom-call(s32[3]{0:T(128)} %add_add_fusion.place_ref, bf16[8,2,1024,128]{3,2,1,0:T(8,128)(2,1)} %all-to-all-done.query_ref, bf16[2048,128]{1,0:T(8,128)(2,1)} %get-tuple-element.38.refs_4_.refs_0_, ...), custom_call_target="tpu_custom_call" | custom-call | flops 2147483648 | bytes 3145728 | tf_op jit(solution)/shard_map/attend_first/pallas_call | solution.py:324
  240.5 2.2 collective-permute-start.22
  243.5 12.1 %collective-permute-start.21 = (bf16[1056,128]{1,0:T(8,128)(2,1)S(1)}, bf16[1056,128]{1,0:T(8,128)(2,1)S(1)}, u32[]{:S(2)}, u32[]{:S(2)}) collective-permute-start(bf16[1056,128]{1,0:T(8,128)(2,1)S(1)} %copy-done.26), channel_id=1, source_target_pairs={{0,6},{2,4},{4,2},{6,0},{8,14},{10,12},{12,10},{14,8},{1,7},{3,5},... | collective-permute-start | bytes 811016 | tf_op jit(solution)/shard_map/ppermute | solution.py:683
  255.6 7.1 %attend_second.5 = (bf16[1056,128]{1,0:T(8,128)(2,1)}, f32[8,128]{1,0:T(8,128)}) custom-call(s32[8]{0:T(128)} %parent_ref.5, s32[3]{0:T(128)} %add_add_fusion.place_ref, bf16[8,2,1024,128]{3,2,1,0:T(8,128)(2,1)} %all-to-all-done.query_ref, bf16[2304,128]{1,0:T(8,128)(2,1)} %get-tuple-element.42.refs_0_, bf16[2304,128]{1,0:T(8,128)(2,1)} %copy-done.10, ...), custom_call_target="tpu_custom_call" | custom-call | flops 1140850688 | bytes 1638400 | tf_op jit(solution)/shard_map/attend_second/pallas_call | solution.py:465
  262.8 0.7 copy-done.15
  263.5 5.2 %merge_parts.2 = bf16[1,128,32,128]{3,2,1,0:T(8,128)(2,1)} custom-call(s32[3]{0:T(128)} %add_add_fusion.place_ref, bf16[1056,128]{1,0:T(8,128)(2,1)} %get-tuple-element.60.refs_0_.refs_9_, bf16[1056,128]{1,0:T(8,128)(2,1)} %copy-done.15, bf16[1056,128]{1,0:T(8,128)(2,1)} %copy-done.13, bf16[1056,128]{1,0:T(8,128)(2,1)} %copy-done.14, ...), custom_call_target="tpu_custom_call" | custom-call | flops 6291456 | bytes 6291456 | tf_op jit(solution)/shard_map/merge_parts/pallas_call | solution.py:631
  269.8 5.2 %merge_parts.3 = bf16[1,128,32,128]{3,2,1,0:T(8,128)(2,1)} custom-call(s32[3]{0:T(128)} %add_add_fusion.place_ref, bf16[1056,128]{1,0:T(8,128)(2,1)} %get-tuple-element.67.refs_0_.refs_9_, bf16[1056,128]{1,0:T(8,128)(2,1)} %copy-done.17, bf16[1056,128]{1,0:T(8,128)(2,1)} %copy-done.18, bf16[1056,128]{1,0:T(8,128)(2,1)} %copy-done.19, ...), custom_call_target="tpu_custom_call" | custom-call | flops 6291456 | bytes 6291456 | tf_op jit(solution)/shard_map/merge_parts/pallas_call | solution.py:631
  (107 shorter events, 5.3 us)
Async XLA Ops:
  6.4 7.4 %copy-start.24 = (s32[8,32]{1,0:T(8,128)S(1)}, s32[8,32]{1,0:T(8,128)}, u32[]{:S(2)}) copy-start(s32[8,32]{1,0:T(8,128)} %param.19) | copy-start | bytes 3076
  6.4 125.6 %all-to-all-start = ((bf16[8,2,1024,128]{3,2,1,0:T(8,128)(2,1)}), bf16[8,2,1024,128]{3,2,1,0:T(8,128)(2,1)}, u32[]{:S(2)}, u32[]{:S(2)}) async-start(bf16[8,2,1024,128]{3,2,1,0:T(8,128)(2,1)} %turn_queries.1.refs_8_.query_ref), calls=%async_computation | async-start | bytes 8388608 | tf_op jit(solution)/shard_map/all_to_all | solution.py:687
  15.5 10.6 %copy-start.22 = (bf16[1,128,4,128]{3,2,1,0:T(4,128)(2,1)S(1)}, bf16[1,128,4,128]{3,2,1,0:T(4,128)(2,1)}, u32[]{:S(2)}) copy-start(bf16[1,128,4,128]{3,2,1,0:T(4,128)(2,1)} %param.12) | copy-start | bytes 393220
  15.5 11.3 %copy-start.11 = (f32[2,128,128]{2,1,0:T(8,128)S(1)}, f32[2,128,128]{2,1,0:T(8,128)}, u32[]{:S(2)}) copy-start(f32[2,128,128]{2,1,0:T(8,128)} %get-tuple-element.84.sine_ref) | copy-start | bytes 393220
  15.5 11.3 %copy-start.12 = (f32[2,128,128]{2,1,0:T(8,128)S(1)}, f32[2,128,128]{2,1,0:T(8,128)}, u32[]{:S(2)}) copy-start(f32[2,128,128]{2,1,0:T(8,128)} %get-tuple-element.85.cosine_ref) | copy-start | bytes 393220
  22.6 81.1 %collective-permute-start.6 = (bf16[4096,128]{1,0:T(8,128)(2,1)}, bf16[4096,128]{1,0:T(8,128)(2,1)S(1)}, u32[]{:S(2)}, u32[]{:S(2)}) collective-permute-start(bf16[4096,128]{1,0:T(8,128)(2,1)} %get-tuple-element.46), channel_id=1, source_target_pairs={{0,2},{2,0},{4,6},{6,4},{8,10},{10,8},{12,14},{14,12},{1,3},{3,1},... | collective-permute-start | bytes 3145736 | tf_op jit(solution)/shard_map/ppermute | solution.py:683
  24.6 82.9 %collective-permute-start.7 = (bf16[4096,128]{1,0:T(8,128)(2,1)}, bf16[4096,128]{1,0:T(8,128)(2,1)S(1)}, u32[]{:S(2)}, u32[]{:S(2)}) collective-permute-start(bf16[4096,128]{1,0:T(8,128)(2,1)} %get-tuple-element.47), channel_id=1, source_target_pairs={{0,4},{2,6},{4,0},{6,2},{8,12},{10,14},{12,8},{14,10},{1,5},{3,7},... | collective-permute-start | bytes 3145736 | tf_op jit(solution)/shard_map/ppermute | solution.py:683
  26.0 104.6 %collective-permute-start.8 = (bf16[4096,128]{1,0:T(8,128)(2,1)}, bf16[4096,128]{1,0:T(8,128)(2,1)S(1)}, u32[]{:S(2)}, u32[]{:S(2)}) collective-permute-start(bf16[4096,128]{1,0:T(8,128)(2,1)} %get-tuple-element.48), channel_id=1, source_target_pairs={{0,6},{2,4},{4,2},{6,0},{8,14},{10,12},{12,10},{14,8},{1,7},{3,5},... | collective-permute-start | bytes 3145736 | tf_op jit(solution)/shard_map/ppermute | solution.py:683
  28.4 11.0 %copy-start.21 = (bf16[1,128,4,128]{3,2,1,0:T(4,128)(2,1)S(1)}, bf16[1,128,4,128]{3,2,1,0:T(4,128)(2,1)}, u32[]{:S(2)}) copy-start(bf16[1,128,4,128]{3,2,1,0:T(4,128)(2,1)} %param.15) | copy-start | bytes 393220
  28.4 11.0 %copy-start.20 = (bf16[1,128,4,128]{3,2,1,0:T(4,128)(2,1)S(1)}, bf16[1,128,4,128]{3,2,1,0:T(4,128)(2,1)}, u32[]{:S(2)}) copy-start(bf16[1,128,4,128]{3,2,1,0:T(4,128)(2,1)} %param.13) | copy-start | bytes 393220
  28.4 11.7 %copy-start.23 = (bf16[1,128,4,128]{3,2,1,0:T(4,128)(2,1)S(1)}, bf16[1,128,4,128]{3,2,1,0:T(4,128)(2,1)}, u32[]{:S(2)}) copy-start(bf16[1,128,4,128]{3,2,1,0:T(4,128)(2,1)} %param.16) | copy-start | bytes 393220
  36.1 61.0 %collective-permute-start.3 = (bf16[2304,128]{1,0:T(8,128)(2,1)}, bf16[2304,128]{1,0:T(8,128)(2,1)S(1)}, u32[]{:S(2)}, u32[]{:S(2)}) collective-permute-start(bf16[2304,128]{1,0:T(8,128)(2,1)} %get-tuple-element.43), channel_id=1, source_target_pairs={{0,2},{2,0},{4,6},{6,4},{8,10},{10,8},{12,14},{14,12},{1,3},{3,1},... | collective-permute-start | bytes 1769480 | tf_op jit(solution)/shard_map/ppermute | solution.py:683
  38.1 111.9 %collective-permute-start.4 = (bf16[2304,128]{1,0:T(8,128)(2,1)}, bf16[2304,128]{1,0:T(8,128)(2,1)}, u32[]{:S(2)}, u32[]{:S(2)}) collective-permute-start(bf16[2304,128]{1,0:T(8,128)(2,1)} %get-tuple-element.44), channel_id=1, source_target_pairs={{0,4},{2,6},{4,0},{6,2},{8,12},{10,14},{12,8},{14,10},{1,5},{3,7},... | collective-permute-start | bytes 1769480 | tf_op jit(solution)/shard_map/ppermute | solution.py:683
  97.0 33.5 %copy-start.10 = (bf16[2304,128]{1,0:T(8,128)(2,1)}, bf16[2304,128]{1,0:T(8,128)(2,1)S(1)}, u32[]{:S(2)}) copy-start(bf16[2304,128]{1,0:T(8,128)(2,1)S(1)} %collective-permute-done.3.refs_1_) | copy-start | bytes 1769476
  97.0 64.7 %collective-permute-start.5 = (bf16[2304,128]{1,0:T(8,128)(2,1)}, bf16[2304,128]{1,0:T(8,128)(2,1)}, u32[]{:S(2)}, u32[]{:S(2)}) collective-permute-start(bf16[2304,128]{1,0:T(8,128)(2,1)} %get-tuple-element.45), channel_id=1, source_target_pairs={{0,6},{2,4},{4,2},{6,0},{8,14},{10,12},{12,10},{14,8},{1,7},{3,5},... | collective-permute-start | bytes 1769480 | tf_op jit(solution)/shard_map/ppermute | solution.py:683
  103.7 28.3 %copy-start = (bf16[4096,128]{1,0:T(8,128)(2,1)}, bf16[4096,128]{1,0:T(8,128)(2,1)S(1)}, u32[]{:S(2)}) copy-start(bf16[4096,128]{1,0:T(8,128)(2,1)S(1)} %collective-permute-done.6.refs_1_.refs_9_) | copy-start | bytes 3145732
  103.7 67.8 %collective-permute-start = (bf16[2048,128]{1,0:T(8,128)(2,1)}, bf16[2048,128]{1,0:T(8,128)(2,1)}, u32[]{:S(2)}, u32[]{:S(2)}) collective-permute-start(bf16[2048,128]{1,0:T(8,128)(2,1)} %get-tuple-element.39), channel_id=1, source_target_pairs={{0,2},{2,0},{4,6},{6,4},{8,10},{10,8},{12,14},{14,12},{1,3},{3,1},... | collective-permute-start | bytes 1572872 | tf_op jit(solution)/shard_map/ppermute | solution.py:683
  107.5 24.5 %copy-start.1 = (bf16[4096,128]{1,0:T(8,128)(2,1)}, bf16[4096,128]{1,0:T(8,128)(2,1)S(1)}, u32[]{:S(2)}) copy-start(bf16[4096,128]{1,0:T(8,128)(2,1)S(1)} %collective-permute-done.7.refs_2_.refs_10_) | copy-start | bytes 3145732
  107.5 70.7 %collective-permute-start.1 = (bf16[2048,128]{1,0:T(8,128)(2,1)}, bf16[2048,128]{1,0:T(8,128)(2,1)}, u32[]{:S(2)}, u32[]{:S(2)}) collective-permute-start(bf16[2048,128]{1,0:T(8,128)(2,1)} %get-tuple-element.40), channel_id=1, source_target_pairs={{0,4},{2,6},{4,0},{6,2},{8,12},{10,14},{12,8},{14,10},{1,5},{3,7},... | collective-permute-start | bytes 1572872 | tf_op jit(solution)/shard_map/ppermute | solution.py:683
  130.6 58.4 %collective-permute-start.2 = (bf16[2048,128]{1,0:T(8,128)(2,1)}, bf16[2048,128]{1,0:T(8,128)(2,1)}, u32[]{:S(2)}, u32[]{:S(2)}) collective-permute-start(bf16[2048,128]{1,0:T(8,128)(2,1)} %get-tuple-element.41), channel_id=1, source_target_pairs={{0,6},{2,4},{4,2},{6,0},{8,14},{10,12},{12,10},{14,8},{1,7},{3,5},... | collective-permute-start | bytes 1572872 | tf_op jit(solution)/shard_map/ppermute | solution.py:683
  137.8 12.2 %copy-start.32 = (bf16[1056,128]{1,0:T(8,128)(2,1)S(1)}, bf16[1056,128]{1,0:T(8,128)(2,1)}, u32[]{:S(2)}) copy-start(bf16[1056,128]{1,0:T(8,128)(2,1)} %get-tuple-element.53) | copy-start | bytes 811012
  150.0 21.5 %copy-start.31 = (bf16[1056,128]{1,0:T(8,128)(2,1)S(1)}, bf16[1056,128]{1,0:T(8,128)(2,1)}, u32[]{:S(2)}) copy-start(bf16[1056,128]{1,0:T(8,128)(2,1)} %get-tuple-element.55) | copy-start | bytes 811012
  150.0 28.3 %copy-start.29 = (bf16[1056,128]{1,0:T(8,128)(2,1)S(1)}, bf16[1056,128]{1,0:T(8,128)(2,1)}, u32[]{:S(2)}) copy-start(bf16[1056,128]{1,0:T(8,128)(2,1)} %get-tuple-element.56) | copy-start | bytes 811012
  150.0 57.1 %collective-permute-start.9 = (bf16[1056,128]{1,0:T(8,128)(2,1)S(1)}, bf16[1056,128]{1,0:T(8,128)(2,1)S(1)}, u32[]{:S(2)}, u32[]{:S(2)}) collective-permute-start(bf16[1056,128]{1,0:T(8,128)(2,1)S(1)} %copy-done.32), channel_id=1, source_target_pairs={{0,8},{2,10},{4,12},{6,14},{8,0},{10,2},{12,4},{14,6},{1,9},{3,11}... | collective-permute-start | bytes 811016 | tf_op jit(solution)/shard_map/ppermute | solution.py:683
  161.7 47.4 %collective-permute-start.10 = (bf16[1056,128]{1,0:T(8,128)(2,1)}, bf16[1056,128]{1,0:T(8,128)(2,1)S(1)}, u32[]{:S(2)}, u32[]{:S(2)}) collective-permute-start(bf16[1056,128]{1,0:T(8,128)(2,1)} %get-tuple-element.54), channel_id=1, source_target_pairs={{0,10},{2,8},{4,14},{6,12},{8,2},{10,0},{12,6},{14,4},{1,11},{3,9}... | collective-permute-start | bytes 811016 | tf_op jit(solution)/shard_map/ppermute | solution.py:683
  171.5 39.4 %collective-permute-start.11 = (bf16[1056,128]{1,0:T(8,128)(2,1)S(1)}, bf16[1056,128]{1,0:T(8,128)(2,1)S(1)}, u32[]{:S(2)}, u32[]{:S(2)}) collective-permute-start(bf16[1056,128]{1,0:T(8,128)(2,1)S(1)} %copy-done.31), channel_id=1, source_target_pairs={{0,12},{2,14},{4,8},{6,10},{8,4},{10,6},{12,0},{14,2},{1,13},{3,15... | collective-permute-start | bytes 811016 | tf_op jit(solution)/shard_map/ppermute | solution.py:683
  178.2 34.8 %collective-permute-start.12 = (bf16[1056,128]{1,0:T(8,128)(2,1)S(1)}, bf16[1056,128]{1,0:T(8,128)(2,1)S(1)}, u32[]{:S(2)}, u32[]{:S(2)}) collective-permute-start(bf16[1056,128]{1,0:T(8,128)(2,1)S(1)} %copy-done.29), channel_id=1, source_target_pairs={{0,14},{2,12},{4,10},{6,8},{8,6},{10,4},{12,2},{14,0},{1,15},{3,13... | collective-permute-start | bytes 811016 | tf_op jit(solution)/shard_map/ppermute | solution.py:683
  189.0 41.6 %collective-permute-start.13 = (bf16[1056,128]{1,0:T(8,128)(2,1)}, bf16[1056,128]{1,0:T(8,128)(2,1)S(1)}, u32[]{:S(2)}, u32[]{:S(2)}) collective-permute-start(bf16[1056,128]{1,0:T(8,128)(2,1)} %get-tuple-element.58), channel_id=1, source_target_pairs={{0,4},{2,6},{4,0},{6,2},{8,12},{10,14},{12,8},{14,10},{1,5},{3,7},... | collective-permute-start | bytes 811016 | tf_op jit(solution)/shard_map/ppermute | solution.py:683
  189.0 18.2 %copy-start.30 = (bf16[1056,128]{1,0:T(8,128)(2,1)S(1)}, bf16[1056,128]{1,0:T(8,128)(2,1)}, u32[]{:S(2)}) copy-start(bf16[1056,128]{1,0:T(8,128)(2,1)} %get-tuple-element.59) | copy-start | bytes 811012
  207.1 9.0 %copy-start.3 = (bf16[1056,128]{1,0:T(8,128)(2,1)}, bf16[1056,128]{1,0:T(8,128)(2,1)S(1)}, u32[]{:S(2)}) copy-start(bf16[1056,128]{1,0:T(8,128)(2,1)S(1)} %collective-permute-done.9.refs_13_.refs_4_) | copy-start | bytes 811012
  207.2 23.5 %collective-permute-start.14 = (bf16[1056,128]{1,0:T(8,128)(2,1)S(1)}, bf16[1056,128]{1,0:T(8,128)(2,1)S(1)}, u32[]{:S(2)}, u32[]{:S(2)}) collective-permute-start(bf16[1056,128]{1,0:T(8,128)(2,1)S(1)} %copy-done.30), channel_id=1, source_target_pairs={{0,6},{2,4},{4,2},{6,0},{8,14},{10,12},{12,10},{14,8},{1,7},{3,5},... | collective-permute-start | bytes 811016 | tf_op jit(solution)/shard_map/ppermute | solution.py:683
  209.2 7.0 %copy-start.4 = (bf16[1056,128]{1,0:T(8,128)(2,1)}, bf16[1056,128]{1,0:T(8,128)(2,1)S(1)}, u32[]{:S(2)}) copy-start(bf16[1056,128]{1,0:T(8,128)(2,1)S(1)} %collective-permute-done.10.refs_14_.refs_5_) | copy-start | bytes 811012
  209.2 33.5 %collective-permute-start.16 = (bf16[1056,128]{1,0:T(8,128)(2,1)}, bf16[1056,128]{1,0:T(8,128)(2,1)S(1)}, u32[]{:S(2)}, u32[]{:S(2)}) collective-permute-start(bf16[1056,128]{1,0:T(8,128)(2,1)} %get-tuple-element.64), channel_id=1, source_target_pairs={{0,8},{2,10},{4,12},{6,14},{8,0},{10,2},{12,4},{14,6},{1,9},{3,11}... | collective-permute-start | bytes 811016 | tf_op jit(solution)/shard_map/ppermute | solution.py:683
  210.9 5.2 %copy-start.5 = (bf16[1056,128]{1,0:T(8,128)(2,1)}, bf16[1056,128]{1,0:T(8,128)(2,1)S(1)}, u32[]{:S(2)}) copy-start(bf16[1056,128]{1,0:T(8,128)(2,1)S(1)} %collective-permute-done.11.refs_15_.refs_6_) | copy-start | bytes 811012
  210.9 32.6 %collective-permute-start.17 = (bf16[1056,128]{1,0:T(8,128)(2,1)}, bf16[1056,128]{1,0:T(8,128)(2,1)S(1)}, u32[]{:S(2)}, u32[]{:S(2)}) collective-permute-start(bf16[1056,128]{1,0:T(8,128)(2,1)} %get-tuple-element.65), channel_id=1, source_target_pairs={{0,10},{2,8},{4,14},{6,12},{8,2},{10,0},{12,6},{14,4},{1,11},{3,9}... | collective-permute-start | bytes 811016 | tf_op jit(solution)/shard_map/ppermute | solution.py:683
  213.1 30.4 %collective-permute-start.18 = (bf16[1056,128]{1,0:T(8,128)(2,1)}, bf16[1056,128]{1,0:T(8,128)(2,1)S(1)}, u32[]{:S(2)}, u32[]{:S(2)}) collective-permute-start(bf16[1056,128]{1,0:T(8,128)(2,1)} %get-tuple-element.66), channel_id=1, source_target_pairs={{0,12},{2,14},{4,8},{6,10},{8,4},{10,6},{12,0},{14,2},{1,13},{3,15... | collective-permute-start | bytes 811016 | tf_op jit(solution)/shard_map/ppermute | solution.py:683
  230.6 9.9 %copy-start.25 = (bf16[1056,128]{1,0:T(8,128)(2,1)S(1)}, bf16[1056,128]{1,0:T(8,128)(2,1)}, u32[]{:S(2)}) copy-start(bf16[1056,128]{1,0:T(8,128)(2,1)} %get-tuple-element.71) | copy-start | bytes 811012
  230.6 12.2 %copy-start.28 = (bf16[1056,128]{1,0:T(8,128)(2,1)S(1)}, bf16[1056,128]{1,0:T(8,128)(2,1)}, u32[]{:S(2)}) copy-start(bf16[1056,128]{1,0:T(8,128)(2,1)} %get-tuple-element.68) | copy-start | bytes 811012
  230.6 12.9 %copy-start.27 = (bf16[1056,128]{1,0:T(8,128)(2,1)S(1)}, bf16[1056,128]{1,0:T(8,128)(2,1)}, u32[]{:S(2)}) copy-start(bf16[1056,128]{1,0:T(8,128)(2,1)} %get-tuple-element.69) | copy-start | bytes 811012
  230.6 12.9 %copy-start.26 = (bf16[1056,128]{1,0:T(8,128)(2,1)S(1)}, bf16[1056,128]{1,0:T(8,128)(2,1)}, u32[]{:S(2)}) copy-start(bf16[1056,128]{1,0:T(8,128)(2,1)} %get-tuple-element.70) | copy-start | bytes 811012
  240.5 22.3 %collective-permute-start.15 = (bf16[1056,128]{1,0:T(8,128)(2,1)}, bf16[1056,128]{1,0:T(8,128)(2,1)S(1)}, u32[]{:S(2)}, u32[]{:S(2)}) collective-permute-start(bf16[1056,128]{1,0:T(8,128)(2,1)} %get-tuple-element.61), channel_id=1, source_target_pairs={{0,2},{2,0},{4,6},{6,4},{8,10},{10,8},{12,14},{14,12},{1,3},{3,1},... | collective-permute-start | bytes 811016 | tf_op jit(solution)/shard_map/ppermute | solution.py:683
  240.5 28.2 %collective-permute-start.22 = (bf16[1056,128]{1,0:T(8,128)(2,1)S(1)}, bf16[1056,128]{1,0:T(8,128)(2,1)S(1)}, u32[]{:S(2)}, u32[]{:S(2)}) collective-permute-start(bf16[1056,128]{1,0:T(8,128)(2,1)S(1)} %copy-done.25), channel_id=1, source_target_pairs={{0,14},{2,12},{4,10},{6,8},{8,6},{10,4},{12,2},{14,0},{1,15},{3,13... | collective-permute-start | bytes 811016 | tf_op jit(solution)/shard_map/ppermute | solution.py:683
  242.7 20.0 %copy-start.7 = (bf16[1056,128]{1,0:T(8,128)(2,1)}, bf16[1056,128]{1,0:T(8,128)(2,1)S(1)}, u32[]{:S(2)}) copy-start(bf16[1056,128]{1,0:T(8,128)(2,1)S(1)} %collective-permute-done.16.refs_19_.refs_4_.refs_13_) | copy-start | bytes 811012
  242.7 26.0 %collective-permute-start.19 = (bf16[1056,128]{1,0:T(8,128)(2,1)S(1)}, bf16[1056,128]{1,0:T(8,128)(2,1)S(1)}, u32[]{:S(2)}, u32[]{:S(2)}) collective-permute-start(bf16[1056,128]{1,0:T(8,128)(2,1)S(1)} %copy-done.28), channel_id=1, source_target_pairs={{0,2},{2,0},{4,6},{6,4},{8,10},{10,8},{12,14},{14,12},{1,3},{3,1},... | collective-permute-start | bytes 811016 | tf_op jit(solution)/shard_map/ppermute | solution.py:683
  243.5 19.3 %copy-start.8 = (bf16[1056,128]{1,0:T(8,128)(2,1)}, bf16[1056,128]{1,0:T(8,128)(2,1)S(1)}, u32[]{:S(2)}) copy-start(bf16[1056,128]{1,0:T(8,128)(2,1)S(1)} %collective-permute-done.17.refs_20_.refs_5_.refs_14_) | copy-start | bytes 811012
  243.5 25.3 %collective-permute-start.20 = (bf16[1056,128]{1,0:T(8,128)(2,1)S(1)}, bf16[1056,128]{1,0:T(8,128)(2,1)S(1)}, u32[]{:S(2)}, u32[]{:S(2)}) collective-permute-start(bf16[1056,128]{1,0:T(8,128)(2,1)S(1)} %copy-done.27), channel_id=1, source_target_pairs={{0,4},{2,6},{4,0},{6,2},{8,12},{10,14},{12,8},{14,10},{1,5},{3,7},... | collective-permute-start | bytes 811016 | tf_op jit(solution)/shard_map/ppermute | solution.py:683
  243.5 19.3 %copy-start.9 = (bf16[1056,128]{1,0:T(8,128)(2,1)}, bf16[1056,128]{1,0:T(8,128)(2,1)S(1)}, u32[]{:S(2)}) copy-start(bf16[1056,128]{1,0:T(8,128)(2,1)S(1)} %collective-permute-done.18.refs_21_.refs_6_.refs_15_) | copy-start | bytes 811012
  243.5 25.3 %collective-permute-start.21 = (bf16[1056,128]{1,0:T(8,128)(2,1)S(1)}, bf16[1056,128]{1,0:T(8,128)(2,1)S(1)}, u32[]{:S(2)}, u32[]{:S(2)}) collective-permute-start(bf16[1056,128]{1,0:T(8,128)(2,1)S(1)} %copy-done.26), channel_id=1, source_target_pairs={{0,6},{2,4},{4,2},{6,0},{8,14},{10,12},{12,10},{14,8},{1,7},{3,5},... | collective-permute-start | bytes 811016 | tf_op jit(solution)/shard_map/ppermute | solution.py:683
  (9 other events, 10.0 us)
